TPU v7x, 32 devices: a whole 2x2x4 slice. The times are simulated.
32 devices in a mesh: lat: 8 (over y, x, core), lon: 4 (over z).
Axes of the slice: x: 2, y: 2, z: 4, core: 2. Of those that a mesh axis runs over, the one named last changes fastest.
Arguments:
- height: float32 [2048, 8640], P('lat', 'lon'), may hold values from -6 to 8
- east_vel: float32 [2048, 8640], P('lat', 'lon'), may hold values from -3 to 3
- north_vel: float32 [2048, 8640], P('lat', 'lon'), may hold values from -3 to 3
- sea_depth: float32 [2048, 8640], P('lat', 'lon'), may hold values from 1 to 4
- sea_mask: int32 [2048, 8640], P('lat', 'lon'), may hold values 0 or 1
- forcing: bfloat16 [2, 8, 2048, 8640], P(None, None, 'lat', 'lon'), may hold values from -6 to 6
- thickness: float32 [8], replicated, may hold values from 1 to 10
- cycle_length: int32 [2048], P('lat'), may hold values from 180 to 720
- slot_order: int32 [720], replicated, may hold values from 0 to 719, each once
- love_index: int32 [720], replicated, may hold values from 0 to 63
- love_table: float32 [64], replicated, may hold values from 0.5 to 1.5
Outputs:
- height_out: float32 [2048, 8640], P('lat', 'lon')
- east_out: float32 [2048, 8640], P('lat', 'lon')
- north_out: float32 [2048, 8640], P('lat', 'lon')
- load_coeffs: float32 [2, 720, 720], P(None, 'lon', 'lat')
- sal_field: float32 [2048, 8640], P('lat', 'lon')
Inputs may be any that keep to these rules, and one draw needn't show every extreme that they name: `slot_order`: every order appears once.
All inputs are finite; a program needn't handle non-finite values. No bound on the sum of `sea_mask` on one device may be relied on, other than what follows from the above.
Results may differ from a plain program's by a relative error of at most 0.014.
Values may be sent and summed in bfloat16 or wider, within the bound.
No kernel may reach another device: no remote copies, remote signals or barrier semaphores. Data moves between devices by JAX's collectives and lax.ppermute only.
A program may use at most 192 MiB of HBM per device.

v0:
```python
import math

import jax
import jax.numpy as jnp
from jax import lax
from jax.sharding import PartitionSpec as P

NLON = 8640
LMAX = 720
LEVELS = 8
ITERS = 10
LOVE_ROWS = 64


time_step = 0.6
drag_coeff = 0.5
tide_speed = 0.1
coriolis_scale = 0.8
degree_block = 24
rescale_limit = 1e20
rescale_log = 20.0 * math.log(10.0)


def padded(block, sides, width, periodic):
    for axis, dim in sides:
        count = lax.axis_size(axis)
        forward = [(i, i + 1) for i in range(count - 1)]
        if periodic:
            forward.append((count - 1, 0))
        backward = [(target, source) for source, target in forward]
        low = lax.ppermute(
            lax.slice_in_dim(block, block.shape[dim] - width, None, axis=dim), axis, forward
        )
        high = lax.ppermute(lax.slice_in_dim(block, 0, width, axis=dim), axis, backward)
        block = jnp.concatenate([low, block, high], axis=dim)
    return block


def cycle_geometry(row_ids, cycle_count):
    latitude = (row_ids.astype(jnp.float32) + 0.5) * (math.pi / cycle_count) - 0.5 * math.pi
    return (jnp.sin(latitude), jnp.cos(latitude))


def start_logs():
    counter = jnp.arange(LMAX).astype(jnp.float32)
    log_terms = jnp.where(
        counter > 0.0, 0.5 * jnp.log((2.0 * counter + 1.0) / jnp.maximum(2.0 * counter, 1.0)), 0.0
    )
    return jnp.cumsum(log_terms)


def next_row(degree, order_col, sine_row, prev_one, prev_two, scale_log):
    deg_gap = degree * degree - order_col * order_col
    past_one = degree >= order_col + 1.0
    past_two = degree >= order_col + 2.0
    lead_sq = jnp.where(
        past_one, (4.0 * degree * degree - 1.0) / jnp.where(past_one, deg_gap, 1.0), 0.0
    )
    lag_num = (2.0 * degree + 1.0) * ((degree - 1.0) * (degree - 1.0) - order_col * order_col)
    lag_sq = jnp.where(
        past_two, lag_num / jnp.where(past_two, (2.0 * degree - 3.0) * deg_gap, 1.0), 0.0
    )
    value_row = jnp.where(
        degree == order_col,
        1.0,
        jnp.sqrt(lead_sq) * sine_row * prev_one - jnp.sqrt(lag_sq) * prev_two,
    )
    large = jnp.abs(value_row) > rescale_limit
    factor = jnp.where(large, 1.0 / rescale_limit, 1.0)
    value_row = value_row * factor
    carried = prev_one * factor
    scale_log = scale_log + jnp.where(large, rescale_log, 0.0)
    output = value_row * jnp.exp(scale_log)
    return (value_row, carried, scale_log, output)


def wave_table(orders, part_ids, lon_ids):
    phases = (orders[:, None] * lon_ids[None, :] % NLON).astype(jnp.float32) * (
        2.0 * math.pi / NLON
    )
    return jnp.where(part_ids[:, None] == 0, jnp.cos(phases), -jnp.sin(phases))


def forward_entries(orders, part_ids, lon_ids):
    return (wave_table(orders, part_ids, lon_ids) / NLON).astype(jnp.bfloat16)


def inverse_entries(orders, part_ids, lon_ids):
    weight_gain = jnp.where(orders == 0, 1.0, 2.0)
    return (weight_gain[:, None] * wave_table(orders, part_ids, lon_ids)).astype(jnp.bfloat16)


def slot_orders(column_ids, per_owner, slot_order):
    owner_ids = column_ids // (2 * per_owner)
    part_ids = column_ids // per_owner % 2
    flat_ids = owner_ids * per_owner + column_ids % per_owner
    matches = flat_ids[:, None] == jnp.arange(LMAX, dtype=jnp.int32)[None, :]
    orders = jnp.sum(jnp.where(matches, slot_order[None, :], 0), axis=1)
    return (orders, part_ids)


def legendre_loop(orders_f, log_m, sines, cosines):
    order_col = orders_f[:, None]
    start_scale = log_m[:, None] + order_col * jnp.log(cosines)[None, :]
    sine_row = sines[None, :]
    empty = jnp.zeros(start_scale.shape, jnp.float32)
    tables = jnp.zeros((orders_f.shape[0], LMAX, sines.shape[0]), jnp.bfloat16)

    def fill_block(block_id, loop_state):
        prev_one, prev_two, scale_log, filled = loop_state
        new_rows = []
        for within in range(degree_block):
            degree = (block_id * degree_block + within).astype(jnp.float32)
            value_row, carried, scale_log, output = next_row(
                degree, order_col, sine_row, prev_one, prev_two, scale_log
            )
            prev_two = carried
            prev_one = value_row
            new_rows.append(output.astype(jnp.bfloat16))
        stacked = jnp.stack(new_rows, axis=1)
        filled = lax.dynamic_update_slice(
            filled,
            stacked,
            (jnp.int32(0), (block_id * degree_block).astype(jnp.int32), jnp.int32(0)),
        )
        return (prev_one, prev_two, scale_log, filled)

    result = lax.fori_loop(0, LMAX // degree_block, fill_block, (empty, empty, start_scale, tables))
    return result[3]


def local(
    height,
    east_vel,
    north_vel,
    sea_depth,
    sea_mask,
    forcing,
    thickness,
    cycle_length,
    slot_order,
    love_index,
    love_table,
):
    lat_rows, lon_cols = height.shape
    lat_parts = lax.axis_size("lat")
    lon_parts = lax.axis_size("lon")
    cycle_count = lat_rows * lat_parts
    per_owner = LMAX // lon_parts
    first_row = lax.axis_index("lat") * lat_rows
    first_col = lax.axis_index("lon") * lon_cols
    row_ids = first_row + jnp.arange(lat_rows, dtype=jnp.int32)
    sines, cosines = cycle_geometry(row_ids, cycle_count)
    inside = (row_ids > 0) & (row_ids < cycle_count - 1)
    wet_cells = jnp.where(inside[:, None] & (sea_mask > 0), 1.0, 0.0).astype(jnp.float32)
    level_weights = thickness / jnp.sum(thickness)
    east_push = jnp.zeros(height.shape, jnp.float32)
    north_push = jnp.zeros(height.shape, jnp.float32)
    for level in range(LEVELS):
        east_push = east_push + level_weights[level] * forcing[0, level].astype(jnp.float32)
        north_push = north_push + level_weights[level] * forcing[1, level].astype(jnp.float32)
    margin = 2 * ITERS
    stacked = jnp.stack([height, east_vel, north_vel, sea_depth, wet_cells, east_push, north_push])
    widened = padded(stacked.astype(jnp.bfloat16), (("lat", 1),), margin, False).astype(
        stacked.dtype
    )
    widened = padded(widened.astype(jnp.bfloat16), (("lon", 2),), margin, True).astype(
        widened.dtype
    )
    wide_rows = first_row - margin + jnp.arange(lat_rows + 2 * margin, dtype=jnp.int32)
    wide_sines, wide_cosines = cycle_geometry(wide_rows, cycle_count)
    coriolis = coriolis_scale * wide_sines[:, None]
    height, east, north = (widened[0], widened[1], widened[2])
    depth_wide, wet_wide, push_east, push_north = (widened[3], widened[4], widened[5], widened[6])
    for substep in range(ITERS):
        east_flux = depth_wide * east
        north_flux = depth_wide * north
        height = height[1:-1, 1:-1] - time_step * wet_wide[1:-1, 1:-1] * (
            0.5
            * (
                east_flux[1:-1, 2:]
                - east_flux[1:-1, :-2]
                + (north_flux[2:, 1:-1] - north_flux[:-2, 1:-1])
            )
        )
        east_slope = 0.5 * (height[1:-1, 2:] - height[1:-1, :-2])
        north_slope = 0.5 * (height[2:, 1:-1] - height[:-2, 1:-1])
        height = height[1:-1, 1:-1]
        east = east[2:-2, 2:-2]
        north = north[2:-2, 2:-2]
        depth_wide = depth_wide[2:-2, 2:-2]
        wet_wide = wet_wide[2:-2, 2:-2]
        push_east = push_east[2:-2, 2:-2]
        push_north = push_north[2:-2, 2:-2]
        coriolis = coriolis[2:-2]
        flow_speed = jnp.sqrt(east * east + north * north + tide_speed * tide_speed)
        damping = 1.0 + time_step * drag_coeff * flow_speed / jnp.where(
            wet_wide > 0.0, depth_wide, 1.0
        )
        east_new = (
            wet_wide * (east + time_step * (coriolis * north - east_slope + push_east)) / damping
        )
        north = (
            wet_wide * (north + time_step * (-coriolis * east - north_slope + push_north)) / damping
        )
        east = east_new
    surface_load = (wet_cells * height).astype(jnp.bfloat16)
    own_lon = first_col + jnp.arange(lon_cols, dtype=jnp.int32)
    column_ids = jnp.arange(2 * per_owner * lax.axis_size("lon"), dtype=jnp.int32)
    orders, part_ids = slot_orders(column_ids, per_owner, slot_order)
    entries = forward_entries(orders, part_ids, own_lon)
    spectra = lax.psum_scatter(
        lax.dot_general(
            entries, surface_load, (((1,), (1,)), ((), ())), preferred_element_type=jnp.float32
        ).astype(jnp.bfloat16),
        "lon",
        scatter_dimension=0,
        tiled=True,
    ).astype(jnp.float32)
    spectra = spectra.reshape(2, per_owner, lat_rows)
    own_orders = lax.dynamic_slice(slot_order, (lax.axis_index("lon") * per_owner,), (per_owner,))
    retained = own_orders[:, None] < cycle_length[None, :]
    weight_lat = 0.5 * cosines * (math.pi / cycle_count)
    weighted = jnp.where(retained[None], spectra * weight_lat[None, None, :], 0.0).astype(
        jnp.bfloat16
    )
    log_starts = start_logs()
    own_logs = jnp.sum(
        jnp.where(
            own_orders[:, None] == jnp.arange(LMAX, dtype=jnp.int32)[None, :],
            log_starts[None, :],
            0.0,
        ),
        axis=1,
    )
    tables = legendre_loop(own_orders.astype(jnp.float32), own_logs, sines, cosines)
    sums = jnp.einsum("knj,pkj->pkn", tables, weighted, preferred_element_type=jnp.float32)
    load_factor = jnp.sum(
        jnp.where(
            love_index[:, None] == jnp.arange(LOVE_ROWS, dtype=jnp.int32)[None, :],
            love_table[None, :],
            0.0,
        ),
        axis=1,
    )
    share_width = LMAX // lat_parts
    report_scale = math.sqrt(NLON * cycle_count)
    sums = lax.psum(sums, "lat")
    coefficients = sums * load_factor[None, None, :]
    scaled = coefficients.astype(jnp.bfloat16)
    own_coeffs = lax.dynamic_slice_in_dim(
        coefficients, lax.axis_index("lat") * share_width, share_width, 2
    )
    load_coeffs = report_scale * own_coeffs
    synthesis = jnp.einsum(
        "knj,pkn->pkj", tables, scaled, preferred_element_type=jnp.float32
    ).astype(jnp.bfloat16)
    synthesis = synthesis.reshape(2 * per_owner, lat_rows)
    shard_rows = lax.all_gather(synthesis, "lon", axis=0, tiled=True)
    column_ids = jnp.arange(shard_rows.shape[0], dtype=jnp.int32)
    orders, part_ids = slot_orders(column_ids, per_owner, slot_order)
    entries = inverse_entries(orders, part_ids, own_lon)
    sal_field = lax.dot_general(
        shard_rows, entries, (((0,), (0,)), ((), ())), preferred_element_type=jnp.float32
    )
    return (height, east, north, load_coeffs, sal_field)


def solution(mesh):
    in_specs = (
        P("lat", "lon"),
        P("lat", "lon"),
        P("lat", "lon"),
        P("lat", "lon"),
        P("lat", "lon"),
        P(None, None, "lat", "lon"),
        P(),
        P("lat"),
        P(),
        P(),
        P(),
    )
    out_specs = (
        P("lat", "lon"),
        P("lat", "lon"),
        P("lat", "lon"),
        P(None, "lon", "lat"),
        P("lat", "lon"),
    )
    return jax.shard_map(local, mesh=mesh, in_specs=in_specs, out_specs=out_specs, check_vma=False)
```

profile of v0, /device:TPU:0, one launch (start us, length us, event | category | flops | bytes accessed | tf_op | source)
XLA Modules:
  0.0 1058.8 jit_solution(18119053795163229721)
XLA Ops:
  16.0 10.8 %bitcast_dynamic-update-slice_fusion.1 = bf16[7,256,2160]{1,2,0:T(8,128)(2,1)S(1)} fusion(bf16[7,256,2160]{1,2,0:T(8,128)(2,1)S(1)} %get-tuple-element.550, bf16[2,8,256,2160]{2,3,1,0:T(8,128)(2,1)} %param.18, f32[]{:T(128)} %bitcast.12, f32[]{:T(128)} %bitcast.11, f32[]{:T(128)} %bitcast.10, f32[]{:T(128)} %bitcast.9, f32[]{:T(128)} %bitcast.8, ...), kind=kLoop, calls=%fused_computation.758 | loop fusion | flops 13271040 | bytes 9953312
  26.8 6.9 bitcast_dynamic-update-slice_fusion
  33.7 4.4 fusion.385
  39.1 4.1 copy.76
  44.5 4.1 copy.75
  48.6 3.1 collective-permute-start
  60.0 3.4 copy.77
  63.4 3.4 copy.78
  66.8 10.5 pad_maximum_fusion
  77.3 4.4 copy-done.7
  81.7 5.1 collective-permute-start.3
  87.6 3.0 collective-permute-done.3
  90.6 4.3 collective-permute-done.2
  94.9 56.4 %concatenate.7 = bf16[7,296,2200]{1,2,0:T(8,128)(2,1)} concatenate(bf16[7,296,20]{1,2,0:T(8,128)(2,1)S(1)} %collective-permute-done.2, bf16[7,296,2160]{1,2,0:T(8,128)(2,1)} %copy-done.7, bf16[7,296,20]{1,2,0:T(8,128)(2,1)S(1)} %collective-permute-done.3), dimensions={2} | concatenate | bytes 18233600 | tf_op jit(solution)/shard_map/concatenate | solution.py:35
  151.3 13.3 %convert_element_type.790 = f32[7,296,2200]{1,2,0:T(8,128)} convert(bf16[7,296,2200]{1,2,0:T(8,128)(2,1)} %concatenate.7) | non-fusion elementwise | flops 4558400 | bytes 27350400 | tf_op jit(solution)/shard_map/convert_element_type | solution.py:167
  164.6 7.3 fusion.354
  171.9 14.8 %slice_bitcast_fusion.1 = (f32[296,2200]{0,1:T(8,128)S(1)}, f32[296,2200]{0,1:T(8,128)}, f32[296,2200]{0,1:T(8,128)}, f32[296,2200]{0,1:T(8,128)}, f32[296,2200]...) fusion(f32[7,296,2200]{1,2,0:T(8,128)} %convert_element_type.790), kind=kLoop, calls=%fused_computation.498 | loop fusion | bytes 36467200 | tf_op jit(solution)/shard_map/squeeze | solution.py:174
  186.7 9.7 fusion.173
  196.4 13.0 %slice_multiply_fusion.11 = (f32[292,2196]{0,1:T(8,128)S(1)}, f32[292,2196]{0,1:T(8,128)}, f32[292,2196]{0,1:T(8,128)}, f32[292,2196]{0,1:T(8,128)}) fusion(f32[296,2200]{0,1:T(8,128)S(1)} %copy-done.3, f32[296,2200]{0,1:T(8,128)S(1)} %get-tuple-element.672, f32[294,2198]{0,1:T(8,128)S(1)} %fusion.173, f32[296,2200]{0,1:T(8,128)} %get-tuple-element.674, ...), kind=kLoop, calls=%fused_computation.711 | loop fusion | flops 18595728 | bytes 35911328 | tf_op jit(solution)/shard_map/mul | solution.py:176
  209.4 8.9 fusion.157
  218.3 19.8 %slice_multiply_fusion.15 = (f32[288,2192]{0,1:T(8,128)}, f32[288,2192]{0,1:T(8,128)}, f32[288,2192]{0,1:T(8,128)}, f32[288,2192]{0,1:T(8,128)}) fusion(f32[296,2200]{0,1:T(8,128)} %get-tuple-element.676, f32[296,2200]{0,1:T(8,128)S(1)} %get-tuple-element.672, f32[290,2194]{0,1:T(8,128)} %fusion.157, f32[292,2196]{0,1:T(8,128)} %get-tuple-element.684, ...), kind=kLoop, calls=%fused_computation.715 | loop fusion | flops 18307584 | bytes 35354880 | tf_op jit(solution)/shard_map/mul | solution.py:176
  238.0 11.0 %fusion.193 = f32[286,2190]{0,1:T(8,128)} fusion(f32[288,2192]{0,1:T(8,128)} %get-tuple-element.681, f32[288,2192]{0,1:T(8,128)} %get-tuple-element.542, f32[296,2200]{0,1:T(8,128)S(1)} %get-tuple-element.677, f32[290,2194]{0,1:T(8,128)} %fusion.157), kind=kLoop, calls=%fused_computation.543 | loop fusion | flops 4384380 | bytes 17537520 | tf_op jit(solution)/shard_map/sub | solution.py:178
  249.0 19.2 %slice_multiply_fusion.13 = (f32[284,2188]{0,1:T(8,128)}, f32[284,2188]{0,1:T(8,128)}, f32[284,2188]{0,1:T(8,128)}, f32[284,2188]{0,1:T(8,128)}) fusion(f32[296,2200]{0,1:T(8,128)} %get-tuple-element.676, f32[296,2200]{0,1:T(8,128)S(1)} %get-tuple-element.672, f32[286,2190]{0,1:T(8,128)} %fusion.193, f32[288,2192]{0,1:T(8,128)} %get-tuple-element.682, ...), kind=kLoop, calls=%fused_computation.713 | loop fusion | flops 18020368 | bytes 34800224 | tf_op jit(solution)/shard_map/mul | solution.py:176
  268.3 9.9 fusion.177
  278.2 12.9 %slice_multiply_fusion.19 = (f32[280,2184]{0,1:T(8,128)}, f32[280,2184]{0,1:T(8,128)}, f32[280,2184]{0,1:T(8,128)}, f32[280,2184]{0,1:T(8,128)}) fusion(f32[296,2200]{0,1:T(8,128)S(1)} %copy-done.4, f32[296,2200]{0,1:T(8,128)S(1)} %get-tuple-element.672, f32[282,2186]{0,1:T(8,128)S(1)} %fusion.177, f32[284,2188]{0,1:T(8,128)} %get-tuple-element.688, ...), kind=kLoop, calls=%fused_computation.719 | loop fusion | flops 17734080 | bytes 34247360 | tf_op jit(solution)/shard_map/mul | solution.py:176
  291.1 9.9 fusion.225
  301.1 12.7 %slice_multiply_fusion.17 = (f32[276,2180]{0,1:T(8,128)S(1)}, f32[276,2180]{0,1:T(8,128)}, f32[276,2180]{0,1:T(8,128)}, f32[276,2180]{0,1:T(8,128)}) fusion(f32[296,2200]{0,1:T(8,128)S(1)} %copy-done.4, f32[296,2200]{0,1:T(8,128)S(1)} %get-tuple-element.672, f32[278,2182]{0,1:T(8,128)S(1)} %fusion.225, f32[280,2184]{0,1:T(8,128)} %get-tuple-element.686, ...), kind=kLoop, calls=%fused_computation.717 | loop fusion | flops 17448720 | bytes 33696288 | tf_op jit(solution)/shard_map/mul | solution.py:176
  313.8 8.8 fusion.209
  322.6 19.4 %slice_multiply_fusion.23 = (f32[272,2176]{0,1:T(8,128)}, f32[272,2176]{0,1:T(8,128)}, f32[272,2176]{0,1:T(8,128)}, f32[272,2176]{0,1:T(8,128)}) fusion(f32[296,2200]{0,1:T(8,128)} %get-tuple-element.676, f32[296,2200]{0,1:T(8,128)S(1)} %get-tuple-element.672, f32[274,2178]{0,1:T(8,128)} %fusion.209, f32[276,2180]{0,1:T(8,128)} %get-tuple-element.692, ...), kind=kLoop, calls=%fused_computation.723 | loop fusion | flops 17164288 | bytes 33147008 | tf_op jit(solution)/shard_map/mul | solution.py:176
  342.0 11.0 %fusion.257 = f32[270,2174]{0,1:T(8,128)} fusion(f32[272,2176]{0,1:T(8,128)} %get-tuple-element.689, f32[272,2176]{0,1:T(8,128)} %get-tuple-element.526, f32[296,2200]{0,1:T(8,128)S(1)} %get-tuple-element.677, f32[274,2178]{0,1:T(8,128)} %fusion.209), kind=kLoop, calls=%fused_computation.639 | loop fusion | flops 4108860 | bytes 16435440 | tf_op jit(solution)/shard_map/sub | solution.py:178
  353.1 19.2 %slice_multiply_fusion.21 = (f32[268,2172]{0,1:T(8,128)}, f32[268,2172]{0,1:T(8,128)}, f32[268,2172]{0,1:T(8,128)}, f32[268,2172]{0,1:T(8,128)}) fusion(f32[296,2200]{0,1:T(8,128)} %get-tuple-element.676, f32[296,2200]{0,1:T(8,128)S(1)} %get-tuple-element.672, f32[270,2174]{0,1:T(8,128)} %fusion.257, f32[272,2176]{0,1:T(8,128)} %get-tuple-element.690, ...), kind=kLoop, calls=%fused_computation.721 | loop fusion | flops 16880784 | bytes 32599520 | tf_op jit(solution)/shard_map/mul | solution.py:176
  372.3 11.1 %fusion.241 = f32[266,2170]{0,1:T(8,128)} fusion(f32[268,2172]{0,1:T(8,128)} %get-tuple-element.695, f32[268,2172]{0,1:T(8,128)} %get-tuple-element.522, f32[296,2200]{0,1:T(8,128)S(1)} %get-tuple-element.677, f32[270,2174]{0,1:T(8,128)} %fusion.257), kind=kLoop, calls=%fused_computation.616 | loop fusion | flops 4040540 | bytes 16162160 | tf_op jit(solution)/shard_map/sub | solution.py:178
  383.4 18.4 %slice_multiply_fusion.27 = (f32[264,2168]{0,1:T(8,128)}, f32[264,2168]{0,1:T(8,128)}, f32[264,2168]{0,1:T(8,128)}, f32[264,2168]{0,1:T(8,128)}) fusion(f32[296,2200]{0,1:T(8,128)} %get-tuple-element.676, f32[296,2200]{0,1:T(8,128)S(1)} %get-tuple-element.672, f32[266,2170]{0,1:T(8,128)} %fusion.241, f32[268,2172]{0,1:T(8,128)} %get-tuple-element.696, ...), kind=kLoop, calls=%fused_computation.727 | loop fusion | flops 16598208 | bytes 32053824 | tf_op jit(solution)/shard_map/mul | solution.py:176
  401.8 11.1 %fusion.289 = f32[262,2166]{0,1:T(8,128)} fusion(f32[264,2168]{0,1:T(8,128)} %get-tuple-element.693, f32[264,2168]{0,1:T(8,128)} %get-tuple-element.518, f32[296,2200]{0,1:T(8,128)S(1)} %get-tuple-element.677, f32[266,2170]{0,1:T(8,128)} %fusion.241), kind=kLoop, calls=%fused_computation.687 | loop fusion | flops 3972444 | bytes 15889776 | tf_op jit(solution)/shard_map/sub | solution.py:178
  413.0 19.2 %slice_multiply_fusion.25 = (f32[260,2164]{0,1:T(8,128)}, f32[260,2164]{0,1:T(8,128)}, f32[260,2164]{0,1:T(8,128)}, f32[260,2164]{0,1:T(8,128)}) fusion(f32[296,2200]{0,1:T(8,128)} %get-tuple-element.676, f32[296,2200]{0,1:T(8,128)S(1)} %get-tuple-element.672, f32[262,2166]{0,1:T(8,128)} %fusion.289, f32[264,2168]{0,1:T(8,128)} %get-tuple-element.694, ...), kind=kLoop, calls=%fused_computation.725 | loop fusion | flops 16316560 | bytes 31509920 | tf_op jit(solution)/shard_map/mul | solution.py:176
  432.2 11.0 %fusion.273 = f32[258,2162]{0,1:T(8,128)} fusion(f32[260,2164]{0,1:T(8,128)} %get-tuple-element.699, f32[260,2164]{0,1:T(8,128)} %get-tuple-element.514, f32[296,2200]{0,1:T(8,128)S(1)} %get-tuple-element.677, f32[262,2166]{0,1:T(8,128)} %fusion.289), kind=kLoop, calls=%fused_computation.664 | loop fusion | flops 3904572 | bytes 15618288 | tf_op jit(solution)/shard_map/sub | solution.py:178
  443.3 15.0 %fusion.307 = (f32[256,2160]{0,1:T(8,128)}, f32[256,2160]{0,1:T(8,128)}, f32[256,2160]{0,1:T(8,128)S(1)}) fusion(f32[296,2200]{0,1:T(8,128)S(1)} %copy-done.2, f32[258,2162]{0,1:T(8,128)} %fusion.273, f32[296,2200]{0,1:T(8,128)} %get-tuple-element.676, f32[260,2164]{0,1:T(8,128)} %get-tuple-element.700, f32[260,2164]{0,1:T(8,128)} %get-tuple-element.515, ...), kind=kLoop, calls=%fused_computation.734 | loop fusion | flops 14929920 | bytes 30967808 | tf_op jit(solution)/shard_map/div | solution.py:204
  459.0 55.8 %fusion.302 = bf16[1440,256]{1,0:T(8,128)(2,1)} fusion(s32[2160]{0:T(1024)S(1)} %copy-done.23, s32[1440]{0:T(1024)S(1)} %copy-done.20, pred[1440]{0:T(1024)(128)(4,1)S(1)} %copy-done.36, bf16[256,2160]{0,1:T(8,128)(2,1)S(1)} %fusion.394), kind=kOutput, calls=%fused_computation.728 | convolution fusion | flops 1633328640 | bytes 1859040 | tf_op jit(solution)/shard_map/dot_general | solution.py:213
  514.9 21.1 %broadcast_in_dim.923.clone = bf16[180,720,256]{2,1,0:T(8,128)(2,1)} broadcast(bf16[]{:T(256)} %constant.625.clone.1), dimensions={} | broadcast | bytes 66355200 | tf_op jit(solution)/shard_map/broadcast_in_dim | solution.py:107
  536.0 330.9 %while.23 = (s32[]{:T(128)}, f32[180,256]{1,0:T(8,128)S(1)}, f32[180,256]{1,0:T(8,128)S(1)}, f32[180,256]{1,0:T(8,128)S(1)}, bf16[180,720,256]{2,1,0:T(8,128)(2,...) while((s32[]{:T(128)}, f32[180,256]{1,0:T(8,128)S(1)}, ...), condition=%wide.region_7.8_spmd.clone, body=%wide.region_6.7_spmd.clone.sunk | while | flops 42912776 | bytes 26192132 | solution.py:128
  545.5 1.9 copy_dynamic-update-slice_fusion.2
  567.5 1.9 copy_dynamic-update-slice_fusion.2
  589.5 1.9 copy_dynamic-update-slice_fusion.2
  600.5 1.9 copy_dynamic-update-slice_fusion.2
  633.4 1.9 copy_dynamic-update-slice_fusion.2
  644.5 1.9 copy_dynamic-update-slice_fusion.2
  655.5 1.9 copy_dynamic-update-slice_fusion.2
  666.6 2.0 copy_dynamic-update-slice_fusion.2
  699.6 1.9 copy_dynamic-update-slice_fusion.2
  721.6 1.9 copy_dynamic-update-slice_fusion.2
  732.7 1.9 copy_dynamic-update-slice_fusion.2
  754.7 1.9 copy_dynamic-update-slice_fusion.2
  765.8 1.9 copy_dynamic-update-slice_fusion.2
  776.8 1.9 copy_dynamic-update-slice_fusion.2
  787.8 1.9 copy_dynamic-update-slice_fusion.2
  809.9 1.9 copy_dynamic-update-slice_fusion.2
  820.9 1.9 copy_dynamic-update-slice_fusion.2
  832.0 1.9 copy_dynamic-update-slice_fusion.2
  865.0 1.9 copy_dynamic-update-slice_fusion.2
  868.1 26.2 %convolution_bitcast_fusion = f32[2,180,720]{2,0,1:T(2,128)} fusion(bf16[180,720,256]{2,1,0:T(8,128)(2,1)} %get-tuple-element.332, f32[2,180,256]{2,1,0:T(8,128)S(1)} %reshape.2027, pred[180,256]{1,0:T(8,128)(4,1)S(1)} %broadcast_compare_fusion, f32[256]{0:T(256)S(1)} %broadcast_multiply_fusion.1), kind=kOutput, calls=%fused_computation.752 | convolution fusion | flops 132986880 | bytes 67807744 | tf_op jit(solution)/shard_map/knj,pkj->pkn/dot_general | solution.py:237
  894.4 56.9 %all-reduce.3.cloned.1.call-done = f32[2,180,720]{2,0,1:T(2,128)} async-done(((f32[2,180,720]{2,0,1:T(2,128)}), f32[2,180,720]{2,0,1:T(2,128)}) %all-reduce.3.cloned.1.call-update) | async-done | bytes 1036816 | tf_op jit(solution)/shard_map/psum | solution.py:248
  952.9 23.5 %fusion.318 = bf16[2,180,256]{2,0,1:T(2,128)(2,1)S(1)} fusion(bf16[180,720,256]{2,1,0:T(8,128)(2,1)} %get-tuple-element.332, f32[2,180,720]{2,0,1:T(2,128)S(1)} %broadcast_multiply_fusion), kind=kOutput, calls=%fused_computation.754 | convolution fusion | flops 133061760 | bytes 67576320 | tf_op jit(solution)/shard_map/knj,pkn->pkj/dot_general | solution.py:255
  977.4 18.6 %all_gather.3 = bf16[1440,256]{1,0:T(8,128)(2,1)S(1)} all-gather(bf16[360,256]{1,0:T(8,128)(2,1)S(1)} %reshape.2023), channel_id=1, replica_groups=mesh['lat'=8,'lon'=4] {'lon'}, dimensions={0}, use_global_device_ids=true | all-gather | bytes 921600 | tf_op jit(solution)/shard_map/all_gather | solution.py:259
  996.0 55.8 %fusion.150 = f32[256,2160]{0,1:T(8,128)} fusion(bf16[1440,256]{1,0:T(8,128)(2,1)S(1)} %all_gather.3, f32[1440]{0:T(1024)S(1)} %compare_select_fusion, s32[2160]{0:T(1024)S(1)} %copy-done.23, s32[1440]{0:T(1024)S(1)} %copy-done.20, pred[1440]{0:T(1024)(128)(4,1)S(1)} %copy-done.36), kind=kOutput, calls=%fused_computation.472 | convolution fusion | flops 1632960000 | bytes 2970720 | tf_op jit(solution)/shard_map/dot_general | solution.py:263
  (1466 shorter events, 310.9 us)
Async XLA Ops:
  7.2 5.2 copy-start.13
  7.2 859.9 %reduce-scatter.2.cloned.1.call-start = ((), (), s32[]{:S(2)}) async-start(), calls=%async_computation.1 | async-start | bytes 921600 | tf_op jit(solution)/shard_map/reduce_scatter | solution.py:212
  9.9 2.6 copy-start.14
  12.4 1.6 copy-start.15
  12.4 2.3 copy-start.16
  12.5 14.3 %copy-start.10 = (bf16[2,8,256,2160]{2,3,1,0:T(8,128)(2,1)S(1)}, bf16[2,8,256,2160]{2,3,1,0:T(8,128)(2,1)}, u32[]{:S(2)}) copy-start(bf16[2,8,256,2160]{2,3,1,0:T(8,128)(2,1)} %param.18) | copy-start | bytes 53084164
  33.7 5.4 copy-start.8
  43.2 12.4 %copy-start.32 = (s32[720]{0:T(1024)S(1)}, s32[720]{0:T(1024)}, u32[]{:S(2)}) copy-start(s32[720]{0:T(1024)} %param.21) | copy-start | bytes 8644
  43.2 20.2 %collective-permute-start.1 = (bf16[7,20,2160]{2,0,1:T(8,128)(2,1)S(1)}, bf16[7,20,2160]{2,0,1:T(8,128)(2,1)S(1)}, u32[]{:S(2)}, u32[]{:S(2)}) collective-permute-start(bf16[7,20,2160]{2,0,1:T(8,128)(2,1)S(1)} %copy.76), channel_id=1, source_target_pairs={{4,0},{8,4},{12,8},{16,12},{20,16},{24,20},{28,24},{5,1},{9,5},{13... | collective-permute-start | bytes 1814408 | tf_op jit(solution)/shard_map/ppermute | solution.py:34
  48.6 11.4 %collective-permute-start = (bf16[7,20,2160]{2,0,1:T(8,128)(2,1)S(1)}, bf16[7,20,2160]{2,0,1:T(8,128)(2,1)S(1)}, u32[]{:S(2)}, u32[]{:S(2)}) collective-permute-start(bf16[7,20,2160]{2,0,1:T(8,128)(2,1)S(1)} %copy.75), channel_id=1, source_target_pairs={{0,4},{4,8},{8,12},{12,16},{16,20},{20,24},{24,28},{1,5},{5,9},{9,... | collective-permute-start | bytes 1814408 | tf_op jit(solution)/shard_map/ppermute | solution.py:31
  56.2 10.6 copy-start.21
  58.3 0.9 copy-start.18
  77.3 4.4 copy-start.7
  81.7 8.9 collective-permute-start.3
  86.8 8.1 collective-permute-start.2
  186.7 9.7 copy-start
  186.7 9.7 copy-start.3
  268.2 9.9 copy-start.1
  268.3 9.9 copy-start.4
  313.7 8.8 copy-start.30
  313.8 8.8 copy-start.31
  342.0 11.0 %copy-start.28 = (f32[268]{0:T(512)S(1)}, f32[268]{0:T(512)}, u32[]{:S(2)}) copy-start(f32[268]{0:T(512)} %get-tuple-element.444) | copy-start | bytes 3220
  342.0 11.0 %copy-start.29 = (f32[268]{0:T(512)S(1)}, f32[268]{0:T(512)}, u32[]{:S(2)}) copy-start(f32[268]{0:T(512)} %get-tuple-element.445) | copy-start | bytes 3220
  372.3 11.1 %copy-start.26 = (f32[264]{0:T(512)S(1)}, f32[264]{0:T(512)}, u32[]{:S(2)}) copy-start(f32[264]{0:T(512)} %get-tuple-element.442) | copy-start | bytes 3172
  372.3 11.1 %copy-start.27 = (f32[264]{0:T(512)S(1)}, f32[264]{0:T(512)}, u32[]{:S(2)}) copy-start(f32[264]{0:T(512)} %get-tuple-element.443) | copy-start | bytes 3172
  401.8 11.2 %copy-start.24 = (f32[260]{0:T(512)S(1)}, f32[260]{0:T(512)}, u32[]{:S(2)}) copy-start(f32[260]{0:T(512)} %get-tuple-element.440) | copy-start | bytes 3124
  401.8 11.2 %copy-start.25 = (f32[260]{0:T(512)S(1)}, f32[260]{0:T(512)}, u32[]{:S(2)}) copy-start(f32[260]{0:T(512)} %get-tuple-element.441) | copy-start | bytes 3124
  432.2 11.0 %copy-start.2 = (f32[296,2200]{0,1:T(8,128)S(1)}, f32[296,2200]{0,1:T(8,128)}, u32[]{:S(2)}) copy-start(f32[296,2200]{0,1:T(8,128)} %get-tuple-element.673) | copy-start | bytes 7814404
  432.2 11.0 %copy-start.33 = (f32[256,1]{0,1:T(1,128)S(1)}, f32[256,1]{0,1:T(1,128)}, u32[]{:S(2)}) copy-start(f32[256,1]{0,1:T(1,128)} %get-tuple-element.706) | copy-start | bytes 3076
  432.2 11.0 %copy-start.34 = (f32[256,1]{0,1:T(1,128)S(1)}, f32[256,1]{0,1:T(1,128)}, u32[]{:S(2)}) copy-start(f32[256,1]{0,1:T(1,128)} %get-tuple-element.707) | copy-start | bytes 3076
  443.2 15.0 %copy-start.12 = (pred[256,2160]{0,1:T(8,128)(4,1)S(1)}, pred[256,2160]{0,1:T(8,128)(4,1)}, u32[]{:S(2)}) copy-start(pred[256,2160]{0,1:T(8,128)(4,1)} %get-tuple-element.551) | copy-start | bytes 1658884
  458.2 56.5 %copy-start.11 = (f32[256,2160]{0,1:T(8,128)}, f32[256,2160]{0,1:T(8,128)S(1)}, u32[]{:S(2)}) copy-start(f32[256,2160]{0,1:T(8,128)S(1)} %get-tuple-element.705) | copy-start | bytes 6635524
  458.2 0.7 copy-start.20
  458.2 0.8 copy-start.23
  458.2 0.8 copy-start.36
  514.8 436.5 %all-reduce.3.cloned.1.call-start = ((), (), s32[]{:S(2)}) async-start(), calls=%async_computation.2 | async-start | bytes 2211840 | tf_op jit(solution)/shard_map/psum | solution.py:248
  514.8 21.1 %copy-start.5 = (f32[180,256]{1,0:T(8,128)S(1)}, f32[180,256]{1,0:T(8,128)}, u32[]{:S(2)}) copy-start(f32[180,256]{1,0:T(8,128)} %custom-call.1) | copy-start | bytes 552964
  514.8 21.1 %copy-start.6 = (f32[180,256]{1,0:T(8,128)S(1)}, f32[180,256]{1,0:T(8,128)}, u32[]{:S(2)}) copy-start(f32[180,256]{1,0:T(8,128)} %custom-call) | copy-start | bytes 552964
  514.8 21.1 %copy-start.9 = (f32[180,256]{1,0:T(8,128)S(1)}, f32[180,256]{1,0:T(8,128)}, u32[]{:S(2)}) copy-start(f32[180,256]{1,0:T(8,128)} %multiply_add_fusion) | copy-start | bytes 552964
  514.9 21.1 %copy-start.17 = (f32[180]{0:T(256)S(1)}, f32[180]{0:T(256)}, u32[]{:S(2)}) copy-start(f32[180]{0:T(256)} %get-tuple-element.512) | copy-start | bytes 2164
  514.9 21.1 %copy-start.19 = (f32[180]{0:T(256)S(1)}, f32[180]{0:T(256)}, u32[]{:S(2)}) copy-start(f32[180]{0:T(256)} %copy-done.18) | copy-start | bytes 2164
  536.0 330.9 %copy-start.22 = (s32[180]{0:T(256)S(1)}, s32[180]{0:T(256)}, u32[]{:S(2)}) copy-start(s32[180]{0:T(256)} %copy-done.21) | copy-start | bytes 2164
  536.0 330.9 %copy-start.37 = (s32[256]{0:T(256)S(1)}, s32[256]{0:T(256)}, u32[]{:S(2)}) copy-start(s32[256]{0:T(256)} %param.20) | copy-start | bytes 3076
  868.0 26.2 %copy-start.35 = (s32[720]{0:T(1024)S(1)}, s32[720]{0:T(1024)}, u32[]{:S(2)}) copy-start(s32[720]{0:T(1024)} %param.22) | copy-start | bytes 8644
  868.0 26.2 %copy-start.38 = (f32[64]{0:T(128)S(1)}, f32[64]{0:T(128)}, u32[]{:S(2)}) copy-start(f32[64]{0:T(128)} %param.23) | copy-start | bytes 772
Sparse Core Ops, SparseCore 0:
  514.9 22.8 reduce-scatter.1
  894.4 56.8 all-reduce.2
where the time goes:
time: 1070 us; the launch traced here: 1060 us
  other arithmetic  604 us (56%)
  local copies, waits for them, and re-layouts  178 us (17%)
  matrix products  161 us (15%)
  waiting for transfers between devices  64.3 us (6%)
  blocking collectives  18.6 us (2%)
  between operations  14.9 us (1%)
    while x690, other arithmetic  226 us
    mul x10, other arithmetic, local(): east_flux = depth_wide * east  161 us
    sub x10, other arithmetic, local(): height[1:-1, 1:-1]  103 us
    psum x1, waiting for transfers between devices, local(): sums = lax.psum(sums, 'lat')  56.9 us
    dynamic_update_slice x30, local copies, waits for them, and re-layouts, fill_block(): lax.dynamic_update_slice(filled, stacked, (jnp.int32(0), (block_id * degr...  56.7 us
    concatenate x1, local copies, waits for them, and re-layouts, padded(): block = jnp.concatenate([low, block, high], axis=dim)  56.4 us
    dot_general x1, matrix products, local(): lax.dot_general(shard_rows, entries, (((0,), (0,)), ((), ())), preferred_...  55.8 us
    dot_general x1, matrix products, local(): lax.dot_general(entries, surface_load, (((1,), (1,)), ((), ())), preferre...  55.8 us
  transfers between devices with their start and end apart: 6, of which 3 were waited for; matrix products, arithmetic and copies ran while one was open for 34% of the time, Pallas kernels for 0%

commit v1 on v0

v1 whole, which is shorter than its diff:
```python
import functools
import math

import jax
import jax.numpy as jnp
import numpy as np
from jax import lax
from jax.experimental import pallas as pl
from jax.experimental.pallas import tpu as pltpu
from jax.sharding import PartitionSpec as P

NLON = 8640
LMAX = 720
LEVELS = 8
ITERS = 10
LOVE_ROWS = 64

time_step = 0.6
drag_coeff = 0.5
tide_speed = 0.1
coriolis_scale = 0.8

MARGIN = 2 * ITERS
STRIP = 24
TOP = 32
BT = 3
FIELDS = 7
GROUP = 8
CHUNK = 32
NCHUNK = -(-LMAX // CHUNK)
CROWS = CHUNK * GROUP
LIMIT = 1e10
SHRINK = 1e-20
SHRINK_LOG = 20.0 * math.log(10.0)
VMEM_LIMIT = 60 * 1024 * 1024


def tile_count(cols):
    tiles = -(-(cols + 2 * STRIP) // 128)
    while cols % tiles or cols // tiles % 8:
        tiles += 1
    return tiles


def wet_of(in_ref, mask):
    return jnp.where((in_ref[...] > 0.0) & (mask > 0), 1.0, 0.0)


def push_of(weight_ref, f_ref, part):
    total = weight_ref[0] * f_ref[part, 0].astype(jnp.float32)
    for level in range(1, LEVELS):
        total += weight_ref[level] * f_ref[part, level].astype(jnp.float32)
    return time_step * total


def edge_kernel(weight_ref, h_ref, e_ref, n_ref, d_ref, m_ref, f_ref, in_ref, out_ref):
    out_ref[0, 0] = 0.3 * h_ref[...]
    out_ref[0, 1] = e_ref[...]
    out_ref[0, 2] = n_ref[...]
    out_ref[0, 3] = d_ref[...]
    out_ref[0, 4] = wet_of(in_ref, m_ref[...])
    out_ref[0, 5] = push_of(weight_ref, f_ref, 0)
    out_ref[0, 6] = push_of(weight_ref, f_ref, 1)


def edges(weights, fields, forcing, inside):
    cols, rows = fields[0].shape
    at = lambda g: g * (cols // STRIP - 1)
    return pl.pallas_call(
        edge_kernel,
        grid=(2,),
        in_specs=[pl.BlockSpec(memory_space=pltpu.SMEM)]
        + [pl.BlockSpec((STRIP, rows), lambda g: (at(g), 0))] * 5
        + [pl.BlockSpec((2, LEVELS, STRIP, rows), lambda g: (0, 0, at(g), 0))]
        + [pl.BlockSpec(inside.shape, lambda g: (0, 0))],
        out_specs=pl.BlockSpec((1, FIELDS, STRIP, rows), lambda g: (g, 0, 0, 0)),
        out_shape=jax.ShapeDtypeStruct((2, FIELDS, STRIP, rows), jnp.float32),
        name="edges",
    )(weights, *fields, forcing, inside)


def push_kernel(weight_ref, f_ref, out_ref):
    out_ref[0] = push_of(weight_ref, f_ref, 0)
    out_ref[1] = push_of(weight_ref, f_ref, 1)


def push(weights, forcing):
    _, _, cols, rows = forcing.shape
    width = 9 * STRIP
    return pl.pallas_call(
        push_kernel,
        grid=(-(-cols // width),),
        in_specs=[
            pl.BlockSpec(memory_space=pltpu.SMEM),
            pl.BlockSpec((2, LEVELS, width, rows), lambda g: (0, 0, g, 0)),
        ],
        out_specs=pl.BlockSpec((2, width, rows), lambda g: (0, g, 0)),
        out_shape=jax.ShapeDtypeStruct((2, cols, rows), jnp.float32),
        compiler_params=pltpu.CompilerParams(vmem_limit_bytes=VMEM_LIMIT),
        cost_estimate=pl.CostEstimate(
            flops=32 * cols * rows, bytes_accessed=40 * cols * rows, transcendentals=0
        ),
        name="push",
    )(weights, forcing)


def arrange_kernel(tiles, h_ref, e_ref, n_ref, d_ref, m_ref, p_ref, halo_ref, in_ref, out_ref):
    lanes = h_ref.shape[0] // tiles
    for t in range(tiles):
        rows = pl.ds(t, lanes, tiles)
        fields = (
            0.3 * h_ref[rows, :], e_ref[rows, :], n_ref[rows, :], d_ref[rows, :],
            wet_of(in_ref, m_ref[rows, :]), p_ref[0, rows, :], p_ref[1, rows, :],
        )
        for v, field in enumerate(fields):
            rest = halo_ref[v, pl.ds(t, 128 - lanes, tiles), :]
            out_ref[v, t] = jnp.concatenate([field, rest], axis=0).T


def arrange(fields, pushes, halo, inside, tiles):
    cols, rows = fields[0].shape
    return pl.pallas_call(
        functools.partial(arrange_kernel, tiles),
        grid=(rows // 128,),
        in_specs=[pl.BlockSpec((cols, 128), lambda g: (0, g))] * 5
        + [pl.BlockSpec((2, cols, 128), lambda g: (0, 0, g))]
        + [pl.BlockSpec(halo.shape[:2] + (128,), lambda g: (0, 0, g))]
        + [pl.BlockSpec((1, 128), lambda g: (0, g))],
        out_specs=pl.BlockSpec((FIELDS, tiles, 128, 128), lambda g: (0, 0, g, 0)),
        out_shape=jax.ShapeDtypeStruct((FIELDS, tiles, rows, 128), jnp.float32),
        compiler_params=pltpu.CompilerParams(vmem_limit_bytes=VMEM_LIMIT),
        name="arrange",
    )(*fields, pushes, halo, inside)


def ocean_kernel(
    nt, field_ref, spin_ref, low_ref, high_ref, ho_ref, eo_ref, no_ref, lo_ref,
    H, E, N, PE, PN, K, D, A, FE, FN,
):
    step = pl.program_id(0)
    block = field_ref.shape[1]
    rows = field_ref.shape[2]
    lanes = ho_ref.shape[0] // nt
    own = slice(TOP, TOP + rows)

    def put(t, where, height, east, north, depth, wet, push_e, push_n):
        is_wet = wet > 0.0
        H[t + 1, where, :] = height
        E[t, where, :] = east
        N[t, where, :] = north
        PE[t, where, :] = push_e
        PN[t, where, :] = push_n
        K[t, where, :] = jnp.where(is_wet, 0.3 / jnp.where(is_wet, depth, 1.0), jnp.inf)
        D[t, where, :] = depth
        A[t, where, :] = jnp.where(is_wet, 0.09, 0.0)
        FE[t + 1, where, :] = depth * east
        FN[t, where, :] = depth * north

    @pl.when(step < nt // block)
    def ingest():
        for b in range(block):
            t = step * block + b
            put(t, own, *[field_ref[v, b] for v in range(FIELDS)])
            put(t, slice(TOP - STRIP, TOP), *[low_ref[v, b] for v in range(FIELDS)])
            put(t, slice(TOP + rows, TOP + rows + STRIP), *[high_ref[v, b] for v in range(FIELDS)])

    @pl.when(step == nt // block - 1)
    def run():
        def close(ref, tiles):
            for r in tiles:
                here = slice(r * 8, r * 8 + 8)
                ref[0, here, :] = pltpu.roll(ref[nt, here, :], 1, 1)
                ref[nt + 1, here, :] = pltpu.roll(ref[1, here, :], 127, 1)

        def substeps(first_tile, last_tile, count):
            tiles = range(first_tile, last_tile)

            def raise_height(t, carry):
                for r in tiles:
                    here = slice(r * 8, r * 8 + 8)
                    slope = FE[t + 2, here, :] - FE[t, here, :]
                    slope = slope + (FN[t, r * 8 + 1 : r * 8 + 9, :] - FN[t, r * 8 - 1 : r * 8 + 7, :])
                    H[t + 1, here, :] = H[t + 1, here, :] - A[t, here, :] * slope
                return carry

            def turn(t, carry):
                for r in tiles:
                    here = slice(r * 8, r * 8 + 8)
                    spin = spin_ref[here, :]
                    slope = H[t + 2, here, :] - H[t, here, :]
                    rise = H[t + 1, r * 8 + 1 : r * 8 + 9, :] - H[t + 1, r * 8 - 1 : r * 8 + 7, :]
                    east, north = E[t, here, :], N[t, here, :]
                    square = east * east + north * north + tide_speed * tide_speed
                    speed = square * lax.rsqrt(square)
                    damp = pl.reciprocal(1.0 + K[t, here, :] * speed, approx=True)
                    east_new = (east + spin * north - slope + PE[t, here, :]) * damp
                    north_new = (north - spin * east - rise + PN[t, here, :]) * damp
                    E[t, here, :] = east_new
                    N[t, here, :] = north_new
                    depth = D[t, here, :]
                    FE[t + 1, here, :] = depth * east_new
                    FN[t, here, :] = depth * north_new
                return carry

            def one(substep, carry):
                close(FE, tiles)
                lax.fori_loop(0, nt, raise_height, 0)
                close(H, tiles)
                lax.fori_loop(0, nt, turn, 0)
                return carry

            lax.fori_loop(0, count, one, 0)

        substep = 0
        while substep < ITERS:
            reach = lambda k: -(-(MARGIN - 2 * k - 1) // 8)
            count = 1
            while substep + count < ITERS and reach(substep + count) == reach(substep):
                count += 1
            substeps(TOP // 8 - reach(substep), (TOP + rows) // 8 + reach(substep), count)
            substep += count

    @pl.when(step >= nt // block - 1)
    def emit():
        first_row = pl.multiple_of(TOP + (step - (nt // block - 1)) * 128, 8)
        here = pl.ds(first_row, 128)
        for t in range(nt):
            where = pl.ds(t, lanes, nt)
            height = H[t + 1, here, :] * (1.0 / 0.3)
            ho_ref[where, :] = height.T[:lanes]
            eo_ref[where, :] = E[t, here, :].T[:lanes]
            no_ref[where, :] = N[t, here, :].T[:lanes]
            lo_ref[:, t * 128 : (t + 1) * 128] = jnp.where(A[t, here, :] > 0.0, height, 0.0).astype(
                jnp.bfloat16
            )


def ocean(cols, fields, spin, low, high):
    _, nt, rows, _ = fields.shape
    block = BT if nt % BT == 0 else 1
    whole = lambda shape: pl.BlockSpec(
        shape, lambda g: (0,) * len(shape), pipeline_mode=pl.Buffered(1)
    )
    steps = nt // block
    by_tile = lambda n: pl.BlockSpec(
        (FIELDS, block, n, 128), lambda g: (0, jnp.minimum(g, steps - 1), 0, 0)
    )
    band = lambda g: jnp.clip(g - (steps - 1), 0, rows // 128 - 1)
    out_block = pl.BlockSpec((cols, 128), lambda g: (0, band(g)))
    load_block = pl.BlockSpec((128, nt * 128), lambda g: (band(g), 0))
    outs = [jax.ShapeDtypeStruct((cols, rows), jnp.float32)] * 3
    outs.append(jax.ShapeDtypeStruct((rows, nt * 128), jnp.bfloat16))
    plain = pltpu.VMEM((nt, TOP + rows + 32, 128), jnp.float32)
    ringed = pltpu.VMEM((nt + 2, TOP + rows + 32, 128), jnp.float32)
    return pl.pallas_call(
        functools.partial(ocean_kernel, nt),
        grid=(steps + rows // 128 - 1,),
        in_specs=[by_tile(rows), whole(spin.shape), by_tile(STRIP), by_tile(STRIP)],
        out_specs=[out_block] * 3 + [load_block],
        out_shape=outs,
        scratch_shapes=[ringed] + [plain] * 7 + [ringed, plain],
        compiler_params=pltpu.CompilerParams(vmem_limit_bytes=VMEM_LIMIT),
        name="ocean",
    )(fields, spin, low, high)


def legendre_kernel(
    start_ref, w_ref, z_ref, s_ref, co_ref, l_ref, y_ref, c_ref, table, one, two, zed, spread
):
    first_block = start_ref[pl.program_id(0)]
    lats = w_ref.shape[2]
    half = lats // 128
    y_ref[...] = jnp.zeros(y_ref.shape, jnp.float32)
    c_ref[...] = jnp.zeros(c_ref.shape, jnp.float32)
    one[...] = jnp.ones(one.shape, jnp.float32)
    two[...] = jnp.ones(two.shape, jnp.float32)
    zed[...] = z_ref[0]
    row_ids = lax.broadcasted_iota(jnp.int32, (4 * GROUP, CROWS), 0)
    lane_ids = lax.broadcasted_iota(jnp.int32, (4 * GROUP, CROWS), 1)
    order_of = lane_ids % GROUP
    match = (row_ids % GROUP == order_of) & (
        row_ids // (2 * GROUP) == (lane_ids // GROUP + order_of) % 2
    )
    chosen = jnp.where(match, 1.0, 0.0)

    def chunk(c, carry):
        pairs = co_ref[0, c]
        for q in range(2 * CHUNK):
            spread[q] = jnp.broadcast_to(pairs[:, q : q + 1], (GROUP, 128))
        for part in range(CHUNK // 16):
            for t in range(half):
                lanes = slice(t * 128, (t + 1) * 128)
                now, old, scale_log = one[:, lanes], two[:, lanes], zed[:, lanes]
                sines = s_ref[:, lanes]
                large = jnp.maximum(jnp.abs(now), jnp.abs(old)) > LIMIT
                factor = jnp.where(large, SHRINK, 1.0)
                now, old = now * factor, old * factor
                scale_log = scale_log + jnp.where(large, SHRINK_LOG, 0.0)
                scale = jnp.exp(scale_log)
                rows = []
                for q in range(part * 16, part * 16 + 16):
                    value = (spread[q] * sines) * now - spread[CHUNK + q] * old
                    old, now = now, value
                    rows.append(value * scale)
                for q in range(0, 16, 2):
                    at = (part * 16 + q) * GROUP
                    table[at : at + 2 * GROUP, lanes] = jnp.concatenate(
                        [rows[q], rows[q + 1]], axis=0
                    ).astype(jnp.bfloat16)
                one[:, lanes], two[:, lanes], zed[:, lanes] = now, old, scale_log
        values = table[...]
        sums = lax.dot_general(
            w_ref[0], values, (((1,), (1,)), ((), ())), preferred_element_type=jnp.float32
        )
        degree_gap = (c * CHUNK - first_block * GROUP) + (lane_ids // GROUP - order_of)
        gain = jnp.where(degree_gap >= 0, chosen, 0.0) * l_ref[c]
        sums = jnp.where(gain != 0.0, sums * gain, 0.0)
        by_part = sums[: 2 * GROUP] + sums[2 * GROUP :]
        for p in range(2):
            c_ref[0, c, p : p + 1, :] = jnp.sum(
                by_part[p * GROUP : (p + 1) * GROUP], axis=0, keepdims=True
            )
        y_ref[0] += jnp.dot(
            sums.astype(jnp.bfloat16), values, preferred_element_type=jnp.float32
        )
        return carry

    first_chunk = jnp.minimum(first_block * GROUP // CHUNK, NCHUNK)
    lax.fori_loop(first_chunk, NCHUNK, chunk, 0)


def legendre(starts, weights, logs, sines, coeffs, loads):
    groups, _, lats = weights.shape
    by_group = lambda x: pl.BlockSpec(
        (1,) + x.shape[1:], lambda g: (g,) + (0,) * (x.ndim - 1)
    )
    whole = lambda x: pl.BlockSpec(x.shape, lambda g: (0,) * x.ndim)
    outs = [
        jax.ShapeDtypeStruct((groups, 4 * GROUP, lats), jnp.float32),
        jax.ShapeDtypeStruct((groups, NCHUNK, 2, CROWS), jnp.float32),
    ]
    return pl.pallas_call(
        legendre_kernel,
        grid=(groups,),
        in_specs=[
            pl.BlockSpec(memory_space=pltpu.SMEM),
            by_group(weights),
            by_group(logs),
            whole(sines),
            by_group(coeffs),
            whole(loads),
        ],
        out_specs=[by_group(x) for x in outs],
        out_shape=outs,
        scratch_shapes=[
            pltpu.VMEM((CROWS, lats), jnp.bfloat16),
            pltpu.VMEM((GROUP, lats), jnp.float32),
            pltpu.VMEM((GROUP, lats), jnp.float32),
            pltpu.VMEM((GROUP, lats), jnp.float32),
            pltpu.VMEM((2 * CHUNK, GROUP, 128), jnp.float32),
        ],
        compiler_params=pltpu.CompilerParams(vmem_limit_bytes=VMEM_LIMIT),
        name="legendre",
    )(starts, weights, logs, sines, coeffs, loads)


def block_of(device, group, devices):
    turned = jnp.where(group % 2 == 0, device, devices - 1 - device)
    return group * devices + turned


def order_layout(devices):
    groups = -(-(LMAX // GROUP) // devices)
    device, group, part, within = np.meshgrid(
        np.arange(devices), np.arange(groups), np.arange(2), np.arange(GROUP), indexing="ij"
    )
    block = group * devices + np.where(group % 2 == 0, device, devices - 1 - device)
    return groups, (block * GROUP + within).reshape(-1), part.reshape(-1)


def sector_table(orders, parts, cols):
    phases = (orders[:, None] * np.arange(cols)[None, :] % NLON) * (2.0 * np.pi / NLON)
    table = np.where(parts[:, None] == 0, np.cos(phases), -np.sin(phases))
    return np.where(orders[:, None] < LMAX, table, 0.0).astype(jnp.bfloat16)


def ring_table(table, tiles):
    ring = np.pad(table, ((0, 0), (0, tiles * 128 - table.shape[1])))
    return ring.reshape(-1, 128, tiles).transpose(0, 2, 1).reshape(ring.shape)


def start_logs():
    t = np.arange(LMAX, dtype=np.float64)
    terms = np.where(t > 0, 0.5 * np.log((2 * t + 1) / np.maximum(2 * t, 1)), 0.0)
    return np.cumsum(terms)


def recurrence(orders):
    degree = jnp.arange(NCHUNK * CHUNK, dtype=jnp.float32).reshape(1, NCHUNK, 1, CHUNK)
    order = orders.astype(jnp.float32)[:, None, :, None]
    gap = degree * degree - order * order
    one, two = degree >= order + 1.0, degree >= order + 2.0
    lead = jnp.where(one, (4.0 * degree * degree - 1.0) / jnp.where(one, gap, 1.0), 0.0)
    lag_num = (2.0 * degree + 1.0) * ((degree - 1.0) * (degree - 1.0) - order * order)
    lag = jnp.where(two, lag_num / jnp.where(two, (2.0 * degree - 3.0) * gap, 1.0), 0.0)
    lead = jnp.sqrt(lead)
    lag = jnp.where(one, jnp.sqrt(lag), -1.0)
    both = jnp.concatenate([lead, lag], axis=3)
    return jnp.pad(both, ((0, 0), (0, 0), (0, 0), (0, 128 - 2 * CHUNK)))


def cycle_geometry(row_ids, cycle_count):
    latitude = (row_ids.astype(jnp.float32) + 0.5) * (math.pi / cycle_count) - 0.5 * math.pi
    return (jnp.sin(latitude), jnp.cos(latitude))


def ring(axis, periodic):
    count = lax.axis_size(axis)
    forward = [(i, i + 1) for i in range(count - 1)]
    if periodic:
        forward.append((count - 1, 0))
    return forward, [(b, a) for a, b in forward]


def local(
    height,
    east_vel,
    north_vel,
    sea_depth,
    sea_mask,
    forcing,
    thickness,
    cycle_length,
    slot_order,
    love_index,
    love_table,
):
    rows, cols = height.shape
    lat_parts, lon_parts = lax.axis_size("lat"), lax.axis_size("lon")
    devices = lat_parts * lon_parts
    cycles = rows * lat_parts
    lat, lon = lax.axis_index("lat"), lax.axis_index("lon")
    bf16, f32 = jnp.bfloat16, jnp.float32

    weights = thickness / jnp.sum(thickness)
    row_ids = lat * rows + jnp.arange(rows, dtype=jnp.int32)
    inside = (row_ids > 0) & (row_ids < cycles - 1)

    tiles = tile_count(cols)
    natural = [x.T for x in (height, east_vel, north_vel, sea_depth, sea_mask)]
    forcing = forcing.transpose(0, 1, 3, 2)
    inside = jnp.where(inside, 1.0, 0.0)[None, :].astype(f32)
    eastward, westward = ring("lon", True)
    northward, southward = ring("lat", False)
    first, last = edges(weights, natural, forcing, inside).astype(bf16)
    left = lax.ppermute(last, "lon", eastward)
    right = lax.ppermute(first, "lon", westward)
    pushes = push(weights, forcing)
    spare = jnp.zeros((FIELDS, tiles * 128 - cols - 2 * STRIP, rows), bf16)
    halo = jnp.concatenate([right, spare, left], axis=1).astype(f32)
    fields = arrange(natural, pushes, halo, inside, tiles)
    low = lax.ppermute(fields[:, :, rows - STRIP :].astype(bf16), "lat", northward).astype(f32)
    high = lax.ppermute(fields[:, :, :STRIP].astype(bf16), "lat", southward).astype(f32)
    wide_rows = lat * rows - TOP + jnp.arange(TOP + rows + 32, dtype=jnp.int32)
    wide_sines, _ = cycle_geometry(wide_rows, cycles)
    spin = (time_step * coriolis_scale) * wide_sines
    spin = jnp.broadcast_to(spin[:, None], (TOP + rows + 32, 128))
    height, east, north, load = ocean(cols, fields, spin, low, high)

    groups, orders, parts = order_layout(devices)
    table = sector_table(orders, parts, cols)
    owned = devices * groups
    orders3 = jnp.asarray(orders.reshape(owned, 2, GROUP)[:, 0], jnp.int32)
    turn = (orders3 * (lon * cols) % NLON).astype(f32) * (2.0 * math.pi / NLON)
    turn_cos, turn_sin = jnp.cos(turn)[:, :, None], jnp.sin(turn)[:, :, None]
    spectra = lax.dot_general(
        jnp.asarray(ring_table(table, tiles)), load, (((1,), (1,)), ((), ())), preferred_element_type=f32
    ).reshape(owned, 2, GROUP, rows)
    spectra = jnp.stack(
        [
            turn_cos * spectra[:, 0] + turn_sin * spectra[:, 1],
            turn_cos * spectra[:, 1] - turn_sin * spectra[:, 0],
        ],
        axis=1,
    )
    _, cosines = cycle_geometry(row_ids, cycles)
    weight_lat = (0.5 / NLON) * cosines * (math.pi / cycles)
    retained = orders3[:, None, :, None] < cycle_length[None, None, None, :]
    weighted = jnp.where(retained, spectra * weight_lat, 0.0).astype(bf16)
    weighted = weighted.reshape(owned * 2 * GROUP, rows)
    mine = lax.psum_scatter(weighted, "lon", scatter_dimension=0, tiled=True)
    mine = lax.all_to_all(mine, "lat", 0, 0, tiled=True)

    mine = mine.reshape(lat_parts, groups * 2 * GROUP, rows)
    flip = jnp.asarray(np.eye(rows)[::-1].astype(bf16))
    hp = lat_parts // 2
    south = mine[:hp].astype(f32)
    north_side = jnp.dot(mine[hp:][::-1], flip, preferred_element_type=f32)
    folded = jnp.stack([south + north_side, south - north_side]).astype(bf16)
    folded = folded.reshape(2, hp, groups, 2 * GROUP, rows).transpose(2, 0, 3, 1, 4)
    folded = folded.reshape(groups, 4 * GROUP, hp * rows)

    device = lon * lat_parts + lat
    starts = jnp.stack([block_of(device, g, devices) for g in range(groups)]).astype(jnp.int32)
    own_orders = starts[:, None] * GROUP + jnp.arange(GROUP, dtype=jnp.int32)[None, :]
    first_logs = jnp.asarray(
        np.pad(start_logs(), (0, owned * GROUP - LMAX)).astype(np.float32)
    )
    own_logs = jnp.stack(
        [lax.dynamic_slice(first_logs, (starts[g] * GROUP,), (GROUP,)) for g in range(groups)]
    )
    half_sines, half_cosines = cycle_geometry(jnp.arange(hp * rows, dtype=jnp.int32), cycles)
    z_start = own_logs[:, :, None] + own_orders.astype(f32)[:, :, None] * jnp.log(half_cosines)
    load_factor = jnp.sum(
        jnp.where(
            love_index[:, None] == jnp.arange(LOVE_ROWS, dtype=jnp.int32)[None, :],
            love_table[None, :],
            0.0,
        ),
        axis=1,
    )
    degree_load = jnp.pad(load_factor, (0, NCHUNK * CHUNK - LMAX)).reshape(NCHUNK, 1, CHUNK, 1)
    degree_load = jnp.broadcast_to(degree_load, (NCHUNK, 1, CHUNK, GROUP)).reshape(NCHUNK, 1, CROWS)
    synth, coeffs = legendre(
        starts,
        folded,
        z_start,
        jnp.broadcast_to(half_sines[None, :], (GROUP, hp * rows)),
        recurrence(own_orders),
        degree_load,
    )

    synth = synth.reshape(groups, 2, 2 * GROUP, hp, rows).transpose(1, 3, 0, 2, 4)
    synth = synth.reshape(2, hp, groups * 2 * GROUP, rows)
    south = (synth[0] + synth[1]).astype(bf16)
    north_side = jnp.dot(
        (synth[0] - synth[1]).astype(bf16), flip, preferred_element_type=f32
    ).astype(bf16)[::-1]
    share = LMAX // lat_parts
    coeffs = coeffs.reshape(groups, NCHUNK, 2, CHUNK, GROUP).transpose(0, 2, 4, 1, 3)
    coeffs = coeffs.reshape(groups * 2 * GROUP, NCHUNK * CHUNK)[:, :LMAX]
    coeffs = coeffs.reshape(groups * 2 * GROUP, lat_parts, share).transpose(1, 0, 2).astype(bf16)
    packet = jnp.concatenate([jnp.concatenate([south, north_side]), coeffs], axis=2)
    packet = lax.all_to_all(packet.reshape(lat_parts * groups * 2 * GROUP, rows + share), "lat", 0, 0, tiled=True)
    packet = lax.all_gather(packet, "lon", axis=0, tiled=True)
    synthesis = packet[:, :rows].reshape(owned, 2, GROUP, rows).astype(f32)

    gain = jnp.where(orders3 == 0, 1.0, 2.0)[:, :, None]
    synthesis = jnp.stack(
        [
            gain * (turn_cos * synthesis[:, 0] - turn_sin * synthesis[:, 1]),
            gain * (turn_sin * synthesis[:, 0] + turn_cos * synthesis[:, 1]),
        ],
        axis=1,
    ).astype(bf16).reshape(owned * 2 * GROUP, rows)
    sal_field = lax.dot_general(
        jnp.asarray(table), synthesis, (((0,), (0,)), ((), ())), preferred_element_type=f32
    )

    per_owner = LMAX // lon_parts
    own_slots = lax.dynamic_slice(slot_order, (lon * per_owner,), (per_owner,))
    found = own_slots[:, None] == orders3.reshape(-1)[None, :]
    by_order = packet[:, rows:].reshape(owned, 2, GROUP, share).transpose(1, 0, 2, 3)
    by_order = by_order.reshape(2, owned * GROUP, share)
    load_coeffs = math.sqrt(NLON * cycles) * jnp.einsum(
        "qm,pmk->pqk", found.astype(bf16), by_order, preferred_element_type=f32
    )
    return (height.T, east.T, north.T, load_coeffs, sal_field.T)


def solution(mesh):
    in_specs = (
        P("lat", "lon"),
        P("lat", "lon"),
        P("lat", "lon"),
        P("lat", "lon"),
        P("lat", "lon"),
        P(None, None, "lat", "lon"),
        P(),
        P("lat"),
        P(),
        P(),
        P(),
    )
    out_specs = (
        P("lat", "lon"),
        P("lat", "lon"),
        P("lat", "lon"),
        P(None, "lon", "lat"),
        P("lat", "lon"),
    )
    return jax.shard_map(local, mesh=mesh, in_specs=in_specs, out_specs=out_specs, check_vma=False)
```

time: 1070 us -> 252 us (0.24)
  other arithmetic: 604 us -> 21.5 us
  local copies, waits for them, and re-layouts: 178 us -> 8.66 us
  matrix products: 161 us -> 13 us
  Pallas kernels: 0 us -> 102 us
    while x690 -> x0, other arithmetic: 226 us -> none
    mul x45 -> x3, other arithmetic: 171 us -> 0.71 us  [the longest x1 0.61 us: local(): starts[:, None] * GROUP + jnp.arange(GROUP, dtype=jnp.int32)[None, :]]
    dot_general x4 -> x5, matrix products: 161 us -> 13 us  [the longest x1 7.02 us: local(): lax.dot_general(jnp.asarray(table), synthesis, (((0,), (0,)), ((), ())),...]
    sub x130 -> x2, other arithmetic: 106 us -> 0.03 us  [the longest x1 0.01 us: recurrence(): 4.0 * degree * degree - 1.0]
    pallas_call x0 -> x5, Pallas kernels: none -> 102 us  [the longest x1 44.9 us: ocean(): pl.pallas_call(functools.partial(ocean_kernel, nt), grid=(steps + rows //...]
    psum x1 -> x0, waiting for transfers between devices: 56.9 us -> none  [local(): sums = lax.psum(sums, 'lat')]
    dynamic_update_slice x30 -> x0, local copies, waits for them, and re-layouts: 56.7 us -> none  [fill_block(): lax.dynamic_update_slice(filled, stacked, (jnp.int32(0), (block_id * degr...]
    concatenate x1, local copies, waits for them, and re-layouts: 56.4 us -> 0.08 us  [local(): halo = jnp.concatenate([right, spare, left], axis=1).astype(f32)]
  transfers between devices with their start and end apart: 6 -> 7, of which waited for: 3 -> 4; matrix products, arithmetic and copies ran while one was open for 34% -> 3% of each run, Pallas kernels for 0% -> 5%
where the time goes in v1:
time: 252 us; the launch traced here: 251 us
  Pallas kernels  102 us (40%)
  waiting for transfers between devices  69.3 us (28%)
  other arithmetic  21.5 us (9%)
  between operations  14.4 us (6%)
  matrix products  13 us (5%)
  starting transfers between devices  11.9 us (5%)
  blocking collectives  10.4 us (4%)
  local copies, waits for them, and re-layouts  8.66 us (3%)
    pallas_call x1, Pallas kernels, ocean(): pl.pallas_call(functools.partial(ocean_kernel, nt), grid=(steps + rows //...  44.9 us
    reduce_scatter x1, waiting for transfers between devices, local(): mine = lax.psum_scatter(weighted, 'lon', scatter_dimension=0, tiled=True)  36.8 us
    pallas_call x1, Pallas kernels, legendre(): pl.pallas_call(legendre_kernel, grid=(groups,), in_specs=[pl.BlockSpec(me...  32 us
    all_gather x1, waiting for transfers between devices, local(): packet = lax.all_gather(packet, 'lon', axis=0, tiled=True)  26.2 us
    pallas_call x1, Pallas kernels, push(): pl.pallas_call(push_kernel, grid=(-(-cols // width),), in_specs=[pl.Block...  12.1 us
    pallas_call x1, Pallas kernels, arrange(): pl.pallas_call(functools.partial(arrange_kernel, tiles), grid=(rows // 12...  11.3 us
    all_to_all x1, blocking collectives, local(): lax.all_to_all(packet.reshape(lat_parts * groups * 2 * GROUP, rows + shar...  10.4 us
    another operation x3, other arithmetic  8.02 us
  transfers between devices with their start and end apart: 7, of which 4 were waited for; matrix products, arithmetic and copies ran while one was open for 3% of the time, Pallas kernels for 5%

profile of v1, /device:TPU:0, one launch (start us, length us, event | category | flops | bytes accessed | tf_op | source)
XLA Modules:
  0.0 251.4 jit_solution(2374037399264702667)
XLA Ops:
  7.2 0.6 and_select_fusion.in_ref
  7.8 1.3 reduce_sum.18
  9.0 1.8 broadcast_divide_fusion.weight_ref
  10.9 2.0 edges.1
  12.8 1.0 convert_element_type.109
  13.8 5.1 %collective-permute-start = (bf16[7,24,256]{2,1,0:T(8,128)(2,1)S(1)}, bf16[7,24,256]{2,1,0:T(8,128)(2,1)S(1)}, u32[]{:S(2)}, u32[]{:S(2)}) collective-permute-start(bf16[7,24,256]{2,1,0:T(8,128)(2,1)S(1)} %get-tuple-element.54), channel_id=1, source_target_pairs={{1,0},{2,1},{3,2},{0,3},{5,4},{6,5},{7,6},{4,7},{9,8},{10,9},{11,1... | collective-permute-start | bytes 258056 | tf_op jit(solution)/shard_map/ppermute | solution.py:457
  19.0 0.1 copy.62
  19.1 0.1 copy.63
  19.2 0.1 select_reduce_fusion
  19.3 0.1 broadcast_in_dim.108
  19.4 0.1 copy.66
  19.5 0.1 pad.28.clone
  19.6 12.1 %push.1.p_ref = f32[2,2160,256]{2,1,0:T(8,128)} custom-call(f32[8]{0:T(128)} %broadcast_divide_fusion.weight_ref, bf16[2,8,2160,256]{3,2,1,0:T(8,128)(2,1)} %bitcast.73), custom_call_target="tpu_custom_call" | custom-call | flops 17694720 | bytes 22118400 | tf_op jit(solution)/shard_map/push/pallas_call | solution.py:90
  31.6 1.1 maximum_convert_fusion.halo_ref
  32.7 11.3 %arrange.1.field_ref = f32[7,18,256,128]{3,2,1,0:T(8,128)} custom-call(f32[2160,256]{1,0:T(8,128)} %bitcast.75, f32[2160,256]{1,0:T(8,128)} %bitcast.77, f32[2160,256]{1,0:T(8,128)} %bitcast.79, f32[2160,256]{1,0:T(8,128)} %bitcast.81, s32[2160,256]{1,0:T(8,128)} %bitcast.83, f32[2,2160,256]{2,1,0:T(8,128)} %push.1.p_ref, ...), custom_call_target="tpu_custom_call" | custom-call | tf_op jit(solution)/shard_map/arrange/pallas_call | solution.py:122
  44.1 6.6 %convert.25 = bf16[7,18,256,128]{3,2,1,0:T(8,128)(2,1)S(1)} convert(f32[7,18,256,128]{3,2,1,0:T(8,128)} %arrange.1.field_ref) | non-fusion elementwise | flops 4128768 | bytes 24772608 | tf_op jit(solution)/shard_map/convert.12
  50.7 0.3 fusion.31
  51.0 1.5 collective-permute-start.2
  52.5 1.3 collective-permute-start.3
  53.9 0.9 dynamic-slice_bitcast_fusion.2
  54.9 0.2 broadcast_compare_fusion
  55.1 1.2 convert_element_type.112.low_ref
  56.3 1.9 collective-permute-done.3
  58.2 1.3 convert_element_type.113.high_ref
  59.4 0.8 broadcast_in_dim.98.spin_ref
  60.2 44.9 %ocean.1 = (f32[2160,256]{1,0:T(8,128)}, f32[2160,256]{1,0:T(8,128)}, f32[2160,256]{1,0:T(8,128)}, bf16[256,2304]{1,0:T(8,128)(2,1)}) custom-call(f32[7,18,256,128]{3,2,1,0:T(8,128)} %arrange.1.field_ref, f32[320,128]{1,0:T(8,128)} %broadcast_in_dim.98.spin_ref, f32[7,18,24,128]{3,2,1,0:T(8,128)} %convert_element_type.112.low_ref, ...), custom_call_target="tpu_custom_call" | custom-call | tf_op jit(solution)/shard_map/ocean/pallas_call | solution.py:255
  105.1 5.4 %fusion.32 = f32[1536,256]{1,0:T(8,128)S(1)} fusion(bf16[1536,2304]{1,0:T(8,128)(2,1)} %constant.111.clone, bf16[256,2304]{1,0:T(8,128)(2,1)} %get-tuple-element.14), kind=kOutput, calls=%fused_computation.82 | convolution fusion | flops 1811939328 | bytes 9830400 | tf_op jit(solution)/shard_map/dot_general | solution.py:476
  110.5 0.3 multiply_add_fusion
  110.8 0.1 pad_maximum_fusion
  110.9 1.1 fusion.1
  112.0 0.6 broadcast_multiply_fusion
  112.7 0.1 add_convert_fusion.1
  112.8 0.1 fusion.30
  112.9 0.7 multiply_add_fusion.1.z_ref
  113.6 0.3 fusion.10
  113.9 36.8 %reduce-scatter.2.cloned.1.call-done = bf16[384,256]{1,0:T(8,128)(2,1)} async-done(((bf16[1536,256]{1,0:T(8,128)(2,1)}), bf16[384,256]{1,0:T(8,128)(2,1)}) %reduce-scatter.2.cloned.1.call-update) | async-done | bytes 196624 | tf_op jit(solution)/shard_map/reduce_scatter | solution.py:491
  150.8 3.7 %all-to-all-start = ((bf16[8,48,256]{2,1,0:T(8,128)(2,1)}), bf16[8,48,256]{2,1,0:T(8,128)(2,1)S(1)}, u32[]{:S(2)}, u32[]{:S(2)}) async-start(bf16[8,48,256]{2,1,0:T(8,128)(2,1)} %bitcast.97), calls=%async_computation.1 | async-start | bytes 393216 | tf_op jit(solution)/shard_map/all_to_all | solution.py:492
  154.5 0.2 all-gather.2.cloned.1.call-start
  154.8 0.7 copy.67.l_ref
  155.5 0.8 select_maximum_fusion.co_ref
  156.3 4.4 %all-to-all-done = bf16[8,48,256]{2,1,0:T(8,128)(2,1)S(1)} async-done(((bf16[8,48,256]{2,1,0:T(8,128)(2,1)}), bf16[8,48,256]{2,1,0:T(8,128)(2,1)S(1)}, u32[]{:S(2)}, u32[]{:S(2)}) %all-to-all-start) | async-done | bytes 196640 | tf_op jit(solution)/shard_map/all_to_all | solution.py:492
  160.8 0.2 fusion.13
  161.1 0.1 maximum_bitcast_fusion
  161.2 0.8 reshape.335.w_ref
  162.0 0.6 broadcast_in_dim.102.s_ref
  162.6 32.0 %legendre.1 = (f32[3,32,1024]{2,1,0:T(8,128)}, f32[3,23,2,256]{3,2,1,0:T(2,128)}) custom-call(s32[3]{0:T(128)} %get-tuple-element.43.start_ref, bf16[3,32,1024]{2,1,0:T(8,128)(2,1)} %reshape.335.w_ref, f32[3,8,1024]{2,1,0:T(8,128)} %multiply_add_fusion.1.z_ref, f32[8,1024]{1,0:T(8,128)} %broadcast_in_dim.102.s_ref, ...), custom_call_target="tpu_custom_call" | custom-call | tf_op jit(solution)/shard_map/legendre/pallas_call | solution.py:342
  194.6 1.0 convert.28
  195.7 0.3 copy.70
  195.9 0.4 copy.71
  196.3 0.2 reshape.341
  196.5 0.1 convert_element_type.125
  196.7 0.2 reshape.339
  196.9 0.1 add_convert_fusion
  197.0 0.2 convolution_convert_fusion
  197.3 10.4 %all_to_all.18 = bf16[8,48,346]{2,1,0:T(8,128)(2,1)} all-to-all(bf16[8,48,346]{2,1,0:T(8,128)(2,1)S(1)} %pad_maximum_fusion.2), channel_id=1, replica_groups=mesh['lat'=8,'lon'=4] {'lat'}, dimensions={0} | all-to-all | bytes 531456 | tf_op jit(solution)/shard_map/all_to_all | solution.py:544
  207.7 0.8 dynamic_slice.15
  208.4 26.2 %all-gather.2.cloned.1.call-done = bf16[1536,346]{1,0:T(8,128)(2,1)} async-done(((bf16[384,346]{1,0:T(8,128)(2,1)}), bf16[1536,346]{1,0:T(8,128)(2,1)}) %all-gather.2.cloned.1.call-update) | async-done | bytes 1062928 | tf_op jit(solution)/shard_map/all_gather | solution.py:545
  234.6 1.2 slice.77
  235.8 0.2 convert.31
  236.1 0.3 fusion.2
  236.4 0.8 copy.75
  237.1 0.4 multiply_convert_fusion.1
  237.5 0.1 pad_maximum_fusion.1
  237.6 7.0 %fusion.33 = f32[256,2160]{0,1:T(8,128)} fusion(bf16[1536,256]{1,0:T(8,128)(2,1)S(1)} %bitcast.90, bf16[1536,2160]{1,0:T(8,128)(2,1)} %constant.114.clone), kind=kOutput, calls=%fused_computation.83 | convolution fusion | flops 1698693120 | bytes 9633792 | tf_op jit(solution)/shard_map/dot_general | solution.py:556
  (49 shorter events, 0.7 us)
Async XLA Ops:
  7.2 143.6 %reduce-scatter.2.cloned.1.call-start = ((), (), s32[]{:S(2)}) async-start(), calls=%async_computation.3 | async-start | bytes 983040 | tf_op jit(solution)/shard_map/reduce_scatter | solution.py:491
  10.9 8.1 %copy-start.4 = (s32[96,8]{0,1:T(8,128)S(1)}, s32[96,8]{0,1:T(8,128)}, u32[]{:S(2)}) copy-start(s32[96,8]{0,1:T(8,128)} %constant.110.clone) | copy-start | bytes 9220
  10.9 8.3 %copy-start.5 = (s32[720]{0:T(1024)S(1)}, s32[720]{0:T(1024)}, u32[]{:S(2)}) copy-start(s32[720]{0:T(1024)} %param.25) | copy-start | bytes 8644
  10.9 8.3 %copy-start.7 = (f32[64]{0:T(128)S(1)}, f32[64]{0:T(128)}, u32[]{:S(2)}) copy-start(f32[64]{0:T(128)} %param.26) | copy-start | bytes 772
  13.8 17.8 %collective-permute-start = (bf16[7,24,256]{2,1,0:T(8,128)(2,1)S(1)}, bf16[7,24,256]{2,1,0:T(8,128)(2,1)S(1)}, u32[]{:S(2)}, u32[]{:S(2)}) collective-permute-start(bf16[7,24,256]{2,1,0:T(8,128)(2,1)S(1)} %get-tuple-element.54), channel_id=1, source_target_pairs={{1,0},{2,1},{3,2},{0,3},{5,4},{6,5},{7,6},{4,7},{9,8},{10,9},{11,1... | collective-permute-start | bytes 258056 | tf_op jit(solution)/shard_map/ppermute | solution.py:457
  19.0 12.7 %collective-permute-start.1 = (bf16[7,24,256]{2,1,0:T(8,128)(2,1)S(1)}, bf16[7,24,256]{2,1,0:T(8,128)(2,1)S(1)}, u32[]{:S(2)}, u32[]{:S(2)}) collective-permute-start(bf16[7,24,256]{2,1,0:T(8,128)(2,1)S(1)} %get-tuple-element.55), channel_id=1, source_target_pairs={{0,1},{1,2},{2,3},{3,0},{4,5},{5,6},{6,7},{7,4},{8,9},{9,10},{10,1... | collective-permute-start | bytes 258056 | tf_op jit(solution)/shard_map/ppermute | solution.py:456
  50.7 4.2 %copy-start.2 = (s32[96,8]{1,0:T(8,128)S(1)}, s32[96,8]{1,0:T(8,128)}, u32[]{:S(2)}) copy-start(s32[96,8]{1,0:T(8,128)} %constant.122) | copy-start | bytes 9220
  50.7 4.2 %copy-start.6 = (s32[256]{0:T(256)S(1)}, s32[256]{0:T(256)}, u32[]{:S(2)}) copy-start(s32[256]{0:T(256)} %param.23) | copy-start | bytes 3076
  51.0 4.1 %collective-permute-start.2 = (bf16[7,18,24,128]{3,2,1,0:T(8,128)(2,1)S(1)}, bf16[7,18,24,128]{3,2,1,0:T(8,128)(2,1)S(1)}, u32[]{:S(2)}, u32[]{:S(2)}) collective-permute-start(bf16[7,18,24,128]{3,2,1,0:T(8,128)(2,1)S(1)} %get-tuple-element.45), channel_id=1, source_target_pairs={{0,4},{4,8},{8,12},{12,16},{16,20},{20,24},{24,28},{1,5},{5,9},{9,... | collective-permute-start | bytes 2322440 | tf_op jit(solution)/shard_map/ppermute | solution.py:462
  52.5 5.7 %collective-permute-start.3 = (bf16[7,18,24,128]{3,2,1,0:T(8,128)(2,1)S(1)}, bf16[7,18,24,128]{3,2,1,0:T(8,128)(2,1)S(1)}, u32[]{:S(2)}, u32[]{:S(2)}) collective-permute-start(bf16[7,18,24,128]{3,2,1,0:T(8,128)(2,1)S(1)} %get-tuple-element.44), channel_id=1, source_target_pairs={{4,0},{8,4},{12,8},{16,12},{20,16},{24,20},{28,24},{5,1},{9,5},{13... | collective-permute-start | bytes 2322440 | tf_op jit(solution)/shard_map/ppermute | solution.py:463
  112.0 48.7 %copy-start = (bf16[256,256,1]{1,0,2:T(8,128)(2,1)S(1)}, bf16[256,256,1]{1,0,2:T(8,128)(2,1)}, u32[]{:S(2)}) copy-start(bf16[256,256,1]{1,0,2:T(8,128)(2,1)} %constant.123) | copy-start | bytes 393220
  150.8 10.0 %all-to-all-start = ((bf16[8,48,256]{2,1,0:T(8,128)(2,1)}), bf16[8,48,256]{2,1,0:T(8,128)(2,1)S(1)}, u32[]{:S(2)}, u32[]{:S(2)}) async-start(bf16[8,48,256]{2,1,0:T(8,128)(2,1)} %bitcast.97), calls=%async_computation.1 | async-start | bytes 393216 | tf_op jit(solution)/shard_map/all_to_all | solution.py:492
  154.5 80.1 %all-gather.2.cloned.1.call-start = ((), (), s32[]{:S(2)}) async-start(), calls=%async_computation.4 | async-start | bytes 1474560 | tf_op jit(solution)/shard_map/all_gather | solution.py:545
  194.6 2.1 copy-start.1
  208.4 27.6 %copy-start.8 = (s32[768]{0:T(1024)S(1)}, s32[768]{0:T(1024)}, u32[]{:S(2)}) copy-start(s32[768]{0:T(1024)} %constant.119) | copy-start | bytes 9220
  234.6 1.5 slice-start
  235.8 1.3 copy-start.3
Sparse Core Ops, SparseCore 0:
  112.2 38.5 reduce-scatter.1
  207.8 26.7 all-gather.1

commit v2 on v1

--- a/solution.py
+++ b/solution.py
@@ -28,6 +28,7 @@
 GROUP = 8
 CHUNK = 32
 NCHUNK = -(-LMAX // CHUNK)
+HELD = NCHUNK + 1
 CROWS = CHUNK * GROUP
 LIMIT = 1e10
 SHRINK = 1e-20
@@ -46,21 +47,22 @@
     return jnp.where((in_ref[...] > 0.0) & (mask > 0), 1.0, 0.0)
 
 
-def push_of(weight_ref, f_ref, part):
-    total = weight_ref[0] * f_ref[part, 0].astype(jnp.float32)
+def push_of(thick_ref, f_ref, part, where=slice(None)):
+    total = thick_ref[0]
+    pushed = total * f_ref[part, 0, where, :].astype(jnp.float32)
     for level in range(1, LEVELS):
-        total += weight_ref[level] * f_ref[part, level].astype(jnp.float32)
-    return time_step * total
-
-
-def edge_kernel(weight_ref, h_ref, e_ref, n_ref, d_ref, m_ref, f_ref, in_ref, out_ref):
-    out_ref[0, 0] = 0.3 * h_ref[...]
-    out_ref[0, 1] = e_ref[...]
-    out_ref[0, 2] = n_ref[...]
-    out_ref[0, 3] = d_ref[...]
-    out_ref[0, 4] = wet_of(in_ref, m_ref[...])
-    out_ref[0, 5] = push_of(weight_ref, f_ref, 0)
-    out_ref[0, 6] = push_of(weight_ref, f_ref, 1)
+        total = total + thick_ref[level]
+        pushed += thick_ref[level] * f_ref[part, level, where, :].astype(jnp.float32)
+    return pushed * (time_step / jnp.full((1, pushed.shape[1]), total, jnp.float32))
+
+
+def edge_kernel(thick_ref, h_ref, e_ref, n_ref, d_ref, m_ref, f_ref, in_ref, out_ref):
+    fields = (
+        0.3 * h_ref[...], e_ref[...], n_ref[...], d_ref[...], wet_of(in_ref, m_ref[...]),
+        push_of(thick_ref, f_ref, 0), push_of(thick_ref, f_ref, 1),
+    )
+    for v, field in enumerate(fields):
+        out_ref[0, v] = field.astype(jnp.bfloat16)
 
 
 def edges(weights, fields, forcing, inside):
@@ -74,19 +76,24 @@
         + [pl.BlockSpec((2, LEVELS, STRIP, rows), lambda g: (0, 0, at(g), 0))]
         + [pl.BlockSpec(inside.shape, lambda g: (0, 0))],
         out_specs=pl.BlockSpec((1, FIELDS, STRIP, rows), lambda g: (g, 0, 0, 0)),
-        out_shape=jax.ShapeDtypeStruct((2, FIELDS, STRIP, rows), jnp.float32),
+        out_shape=jax.ShapeDtypeStruct((2, FIELDS, STRIP, rows), jnp.bfloat16),
         name="edges",
     )(weights, *fields, forcing, inside)
 
 
-def push_kernel(weight_ref, f_ref, out_ref):
-    out_ref[0] = push_of(weight_ref, f_ref, 0)
-    out_ref[1] = push_of(weight_ref, f_ref, 1)
+def push_kernel(thick_ref, f_ref, out_ref):
+    def part(i, carry):
+        where = pl.ds(pl.multiple_of(i * STRIP, 8), STRIP)
+        out_ref[0, where, :] = push_of(thick_ref, f_ref, 0, where)
+        out_ref[1, where, :] = push_of(thick_ref, f_ref, 1, where)
+        return carry
+
+    lax.fori_loop(0, out_ref.shape[1] // STRIP, part, 0)
 
 
 def push(weights, forcing):
     _, _, cols, rows = forcing.shape
-    width = 9 * STRIP
+    width = 15 * STRIP
     return pl.pallas_call(
         push_kernel,
         grid=(-(-cols // width),),
@@ -104,9 +111,21 @@
     )(weights, forcing)
 
 
-def arrange_kernel(tiles, h_ref, e_ref, n_ref, d_ref, m_ref, p_ref, halo_ref, in_ref, out_ref):
+def arrange_kernel(
+    tiles, h_ref, e_ref, n_ref, d_ref, m_ref, p_ref, east_ref, west_ref, in_ref,
+    out_ref, first_ref, last_ref, halo_ref,
+):
     lanes = h_ref.shape[0] // tiles
-    for t in range(tiles):
+
+    @pl.when(pl.program_id(0) == 0)
+    def start():
+        halo_ref[...] = jnp.zeros(halo_ref.shape, jnp.float32)
+        for v in range(FIELDS):
+            halo_ref[v, :STRIP, :] = east_ref[v].astype(jnp.float32)
+            halo_ref[v, halo_ref.shape[1] - STRIP :, :] = west_ref[v].astype(jnp.float32)
+
+    for b in range(out_ref.shape[1]):
+        t = pl.program_id(0) * out_ref.shape[1] + b
         rows = pl.ds(t, lanes, tiles)
         fields = (
             0.3 * h_ref[rows, :], e_ref[rows, :], n_ref[rows, :], d_ref[rows, :],
@@ -114,34 +133,44 @@
         )
         for v, field in enumerate(fields):
             rest = halo_ref[v, pl.ds(t, 128 - lanes, tiles), :]
-            out_ref[v, t] = jnp.concatenate([field, rest], axis=0).T
-
-
-def arrange(fields, pushes, halo, inside, tiles):
+            turned = jnp.concatenate([field, rest], axis=0).T
+            out_ref[v, b] = turned
+            first_ref[v, b] = turned[:STRIP].astype(jnp.bfloat16)
+            last_ref[v, b] = turned[128 - STRIP :].astype(jnp.bfloat16)
+
+
+def arrange(fields, pushes, east, west, inside, tiles, at):
     cols, rows = fields[0].shape
+    block = BT if tiles % BT == 0 else 1
+    edge = jax.ShapeDtypeStruct((FIELDS, tiles, STRIP, 128), jnp.bfloat16)
+    out_block = lambda n: pl.BlockSpec((FIELDS, block, n, 128), lambda g: (0, g, 0, 0))
+    halo_block = pl.BlockSpec((FIELDS, STRIP, 128), lambda g: (0, 0, at))
     return pl.pallas_call(
         functools.partial(arrange_kernel, tiles),
-        grid=(rows // 128,),
-        in_specs=[pl.BlockSpec((cols, 128), lambda g: (0, g))] * 5
-        + [pl.BlockSpec((2, cols, 128), lambda g: (0, 0, g))]
-        + [pl.BlockSpec(halo.shape[:2] + (128,), lambda g: (0, 0, g))]
-        + [pl.BlockSpec((1, 128), lambda g: (0, g))],
-        out_specs=pl.BlockSpec((FIELDS, tiles, 128, 128), lambda g: (0, 0, g, 0)),
-        out_shape=jax.ShapeDtypeStruct((FIELDS, tiles, rows, 128), jnp.float32),
+        grid=(tiles // block,),
+        in_specs=[pl.BlockSpec((cols, 128), lambda g: (0, at))] * 5
+        + [pl.BlockSpec((2, cols, 128), lambda g: (0, 0, at))]
+        + [halo_block] * 2
+        + [pl.BlockSpec((1, 128), lambda g: (0, at))],
+        out_specs=[out_block(128), out_block(STRIP), out_block(STRIP)],
+        out_shape=[jax.ShapeDtypeStruct((FIELDS, tiles, 128, 128), jnp.float32), edge, edge],
+        scratch_shapes=[pltpu.VMEM((FIELDS, tiles * 128 - cols, 128), jnp.float32)],
         compiler_params=pltpu.CompilerParams(vmem_limit_bytes=VMEM_LIMIT),
+        cost_estimate=pl.CostEstimate(
+            flops=64 * cols * 128, bytes_accessed=64 * cols * 128, transcendentals=0
+        ),
         name="arrange",
-    )(*fields, pushes, halo, inside)
-
-
-def ocean_kernel(
-    nt, field_ref, spin_ref, low_ref, high_ref, ho_ref, eo_ref, no_ref, lo_ref,
-    H, E, N, PE, PN, K, D, A, FE, FN,
-):
+    )(*fields, pushes, east, west, inside)
+
+
+def ocean_kernel(nt, parts, *refs):
+    field_refs, refs = refs[:parts], refs[parts:]
+    spin_ref, low_ref, high_ref, ho_ref, eo_ref, no_ref, lo_ref, *refs = refs
+    H, E, N, PE, PN, K, D, A, FE, FN = refs
     step = pl.program_id(0)
-    block = field_ref.shape[1]
-    rows = field_ref.shape[2]
+    block = field_refs[0].shape[1]
+    rows = parts * 128
     lanes = ho_ref.shape[0] // nt
-    own = slice(TOP, TOP + rows)
 
     def put(t, where, height, east, north, depth, wet, push_e, push_n):
         is_wet = wet > 0.0
@@ -160,9 +189,11 @@
     def ingest():
         for b in range(block):
             t = step * block + b
-            put(t, own, *[field_ref[v, b] for v in range(FIELDS)])
-            put(t, slice(TOP - STRIP, TOP), *[low_ref[v, b] for v in range(FIELDS)])
-            put(t, slice(TOP + rows, TOP + rows + STRIP), *[high_ref[v, b] for v in range(FIELDS)])
+            for part, ref in enumerate(field_refs):
+                where = slice(TOP + part * 128, TOP + (part + 1) * 128)
+                put(t, where, *[ref[v, b] for v in range(FIELDS)])
+            put(t, slice(TOP - STRIP, TOP), *[low_ref[v, b].astype(jnp.float32) for v in range(FIELDS)])
+            put(t, slice(TOP + rows, TOP + rows + STRIP), *[high_ref[v, b].astype(jnp.float32) for v in range(FIELDS)])
 
     @pl.when(step == nt // block - 1)
     def run():
@@ -236,7 +267,7 @@
 
 
 def ocean(cols, fields, spin, low, high):
-    _, nt, rows, _ = fields.shape
+    nt, rows = fields[0].shape[1], 128 * len(fields)
     block = BT if nt % BT == 0 else 1
     whole = lambda shape: pl.BlockSpec(
         shape, lambda g: (0,) * len(shape), pipeline_mode=pl.Buffered(1)
@@ -253,25 +284,28 @@
     plain = pltpu.VMEM((nt, TOP + rows + 32, 128), jnp.float32)
     ringed = pltpu.VMEM((nt + 2, TOP + rows + 32, 128), jnp.float32)
     return pl.pallas_call(
-        functools.partial(ocean_kernel, nt),
+        functools.partial(ocean_kernel, nt, len(fields)),
         grid=(steps + rows // 128 - 1,),
-        in_specs=[by_tile(rows), whole(spin.shape), by_tile(STRIP), by_tile(STRIP)],
+        in_specs=[by_tile(128)] * len(fields) + [whole(spin.shape), by_tile(STRIP), by_tile(STRIP)],
         out_specs=[out_block] * 3 + [load_block],
         out_shape=outs,
         scratch_shapes=[ringed] + [plain] * 7 + [ringed, plain],
         compiler_params=pltpu.CompilerParams(vmem_limit_bytes=VMEM_LIMIT),
         name="ocean",
-    )(fields, spin, low, high)
+    )(*fields, spin, low, high)
 
 
 def legendre_kernel(
-    start_ref, w_ref, z_ref, s_ref, co_ref, l_ref, y_ref, c_ref, table, one, two, zed, spread
+    start_ref, w_ref, z_ref, s_ref, co_ref, l_ref, y_ref, c_ref,
+    table_a, table_b, partial_a, partial_b, one, two, zed, scales, folded, spread,
 ):
     first_block = start_ref[pl.program_id(0)]
     lats = w_ref.shape[2]
     half = lats // 128
     y_ref[...] = jnp.zeros(y_ref.shape, jnp.float32)
     c_ref[...] = jnp.zeros(c_ref.shape, jnp.float32)
+    table_b[...] = jnp.zeros(table_b.shape, jnp.bfloat16)
+    partial_b[...] = jnp.zeros(partial_b.shape, jnp.float32)
     one[...] = jnp.ones(one.shape, jnp.float32)
     two[...] = jnp.ones(two.shape, jnp.float32)
     zed[...] = z_ref[0]
@@ -282,51 +316,101 @@
         row_ids // (2 * GROUP) == (lane_ids // GROUP + order_of) % 2
     )
     chosen = jnp.where(match, 1.0, 0.0)
-
-    def chunk(c, carry):
+    first_part = (row_ids // GROUP) % 2 == 0
+    degree_of = (lane_ids // GROUP - order_of - first_block * GROUP)[:1]
+    is_even = lax.broadcasted_iota(jnp.int32, (GROUP, lats), 0) % 2 == 0
+    for p in range(2):
+        even = w_ref[0, p * GROUP : (p + 1) * GROUP, :]
+        odd = w_ref[0, (2 + p) * GROUP : (3 + p) * GROUP, :]
+        folded[0, p] = jnp.where(is_even, even, odd)
+        folded[1, p] = jnp.where(is_even, odd, even)
+
+    def build(c, table, partial, between):
         pairs = co_ref[0, c]
         for q in range(2 * CHUNK):
             spread[q] = jnp.broadcast_to(pairs[:, q : q + 1], (GROUP, 128))
+        tiles = [slice(t * 128, (t + 1) * 128) for t in range(half)]
         for part in range(CHUNK // 16):
-            for t in range(half):
-                lanes = slice(t * 128, (t + 1) * 128)
-                now, old, scale_log = one[:, lanes], two[:, lanes], zed[:, lanes]
-                sines = s_ref[:, lanes]
-                large = jnp.maximum(jnp.abs(now), jnp.abs(old)) > LIMIT
+            between(part)
+            now, old = [one[:, x] for x in tiles], [two[:, x] for x in tiles]
+            for t, lanes in enumerate(tiles):
+                large = jnp.maximum(jnp.abs(now[t]), jnp.abs(old[t])) > LIMIT
                 factor = jnp.where(large, SHRINK, 1.0)
-                now, old = now * factor, old * factor
-                scale_log = scale_log + jnp.where(large, SHRINK_LOG, 0.0)
-                scale = jnp.exp(scale_log)
-                rows = []
-                for q in range(part * 16, part * 16 + 16):
-                    value = (spread[q] * sines) * now - spread[CHUNK + q] * old
-                    old, now = now, value
-                    rows.append(value * scale)
-                for q in range(0, 16, 2):
-                    at = (part * 16 + q) * GROUP
-                    table[at : at + 2 * GROUP, lanes] = jnp.concatenate(
-                        [rows[q], rows[q + 1]], axis=0
-                    ).astype(jnp.bfloat16)
-                one[:, lanes], two[:, lanes], zed[:, lanes] = now, old, scale_log
-        values = table[...]
-        sums = lax.dot_general(
-            w_ref[0], values, (((1,), (1,)), ((), ())), preferred_element_type=jnp.float32
+                now[t], old[t] = now[t] * factor, old[t] * factor
+                scale_log = zed[:, lanes] + jnp.where(large, SHRINK_LOG, 0.0)
+                zed[:, lanes] = scale_log
+                scales[:, lanes] = jnp.exp(scale_log)
+            before = None
+            for q in range(part * 16, part * 16 + 16):
+                lead, lag = spread[q], spread[CHUNK + q]
+                totals, rows = [None, None], []
+                for t, lanes in enumerate(tiles):
+                    value = (lead * s_ref[:, lanes]) * now[t] - lag * old[t]
+                    old[t], now[t] = now[t], value
+                    value = value * scales[:, lanes]
+                    rows.append(value)
+                    for p in range(2):
+                        term = value * folded[q % 2, p, :, lanes]
+                        totals[p] = term if t == 0 else totals[p] + term
+                for p in range(2):
+                    partial[p, q * GROUP : (q + 1) * GROUP, :] = totals[p]
+                if q % 2:
+                    for t, lanes in enumerate(tiles):
+                        table[(q - 1) * GROUP : (q + 1) * GROUP, lanes] = jnp.concatenate(
+                            [before[t], rows[t]], axis=0
+                        ).astype(jnp.bfloat16)
+                before = rows
+            for t, lanes in enumerate(tiles):
+                one[:, lanes], two[:, lanes] = now[t], old[t]
+
+    def sums_of(c, partial):
+        ones = jnp.ones((GROUP, 128), jnp.bfloat16)
+        across = lambda x: lax.dot_general(
+            ones, x, (((1,), (1,)), ((), ())), preferred_element_type=jnp.float32
         )
-        degree_gap = (c * CHUNK - first_block * GROUP) + (lane_ids // GROUP - order_of)
-        gain = jnp.where(degree_gap >= 0, chosen, 0.0) * l_ref[c]
-        sums = jnp.where(gain != 0.0, sums * gain, 0.0)
-        by_part = sums[: 2 * GROUP] + sums[2 * GROUP :]
+        gain = jnp.where(degree_of + c * CHUNK >= 0, l_ref[c], 0.0)
+        sums = []
         for p in range(2):
-            c_ref[0, c, p : p + 1, :] = jnp.sum(
-                by_part[p * GROUP : (p + 1) * GROUP], axis=0, keepdims=True
-            )
-        y_ref[0] += jnp.dot(
-            sums.astype(jnp.bfloat16), values, preferred_element_type=jnp.float32
-        )
+            high = partial[p].astype(jnp.bfloat16)
+            low = (partial[p] - high.astype(jnp.float32)).astype(jnp.bfloat16)
+            total = (across(high) + across(low))[:1]
+            total = jnp.where(gain != 0.0, total * gain, 0.0)
+            c_ref[0, c, p : p + 1, :] = total
+            sums.append(total)
+        return (jnp.where(first_part, sums[0], sums[1]) * chosen).astype(jnp.bfloat16)
+
+    def user(c, table, partial):
+        held = []
+        count = CHUNK // 16 - 1
+
+        def piece(part):
+            if part == 0:
+                held.append(sums_of(c, partial))
+            else:
+                width = lats // count
+                lanes = slice((part - 1) * width, part * width)
+                y_ref[0, :, lanes] += jnp.dot(
+                    held[0], table[:, lanes], preferred_element_type=jnp.float32
+                )
+
+        return piece
+
+    first_chunk = first_block * GROUP // CHUNK
+
+    def pair(i, carry):
+        c = first_chunk + 2 * i
+        build(c, table_a, partial_a, user(jnp.maximum(c - 1, 0), table_b, partial_b))
+        build(c + 1, table_b, partial_b, user(c, table_a, partial_a))
         return carry
 
-    first_chunk = jnp.minimum(first_block * GROUP // CHUNK, NCHUNK)
-    lax.fori_loop(first_chunk, NCHUNK, chunk, 0)
+    count = jnp.maximum(NCHUNK - first_chunk + 1, 0) // 2
+    lax.fori_loop(0, count, pair, 0)
+
+    @pl.when(count > 0)
+    def last():
+        piece = user(first_chunk + 2 * count - 1, table_b, partial_b)
+        for part in range(CHUNK // 16):
+            piece(part)
 
 
 def legendre(starts, weights, logs, sines, coeffs, loads):
@@ -337,7 +421,7 @@
     whole = lambda x: pl.BlockSpec(x.shape, lambda g: (0,) * x.ndim)
     outs = [
         jax.ShapeDtypeStruct((groups, 4 * GROUP, lats), jnp.float32),
-        jax.ShapeDtypeStruct((groups, NCHUNK, 2, CROWS), jnp.float32),
+        jax.ShapeDtypeStruct((groups, HELD, 2, CROWS), jnp.float32),
     ]
     return pl.pallas_call(
         legendre_kernel,
@@ -354,9 +438,14 @@
         out_shape=outs,
         scratch_shapes=[
             pltpu.VMEM((CROWS, lats), jnp.bfloat16),
+            pltpu.VMEM((CROWS, lats), jnp.bfloat16),
+            pltpu.VMEM((2, CROWS, 128), jnp.float32),
+            pltpu.VMEM((2, CROWS, 128), jnp.float32),
             pltpu.VMEM((GROUP, lats), jnp.float32),
             pltpu.VMEM((GROUP, lats), jnp.float32),
             pltpu.VMEM((GROUP, lats), jnp.float32),
+            pltpu.VMEM((GROUP, lats), jnp.float32),
+            pltpu.VMEM((2, 2, GROUP, lats), jnp.float32),
             pltpu.VMEM((2 * CHUNK, GROUP, 128), jnp.float32),
         ],
         compiler_params=pltpu.CompilerParams(vmem_limit_bytes=VMEM_LIMIT),
@@ -396,7 +485,7 @@
 
 
 def recurrence(orders):
-    degree = jnp.arange(NCHUNK * CHUNK, dtype=jnp.float32).reshape(1, NCHUNK, 1, CHUNK)
+    degree = jnp.arange(HELD * CHUNK, dtype=jnp.float32).reshape(1, HELD, 1, CHUNK)
     order = orders.astype(jnp.float32)[:, None, :, None]
     gap = degree * degree - order * order
     one, two = degree >= order + 1.0, degree >= order + 2.0
@@ -442,7 +531,6 @@
     lat, lon = lax.axis_index("lat"), lax.axis_index("lon")
     bf16, f32 = jnp.bfloat16, jnp.float32
 
-    weights = thickness / jnp.sum(thickness)
     row_ids = lat * rows + jnp.arange(rows, dtype=jnp.int32)
     inside = (row_ids > 0) & (row_ids < cycles - 1)
 
@@ -452,15 +540,15 @@
     inside = jnp.where(inside, 1.0, 0.0)[None, :].astype(f32)
     eastward, westward = ring("lon", True)
     northward, southward = ring("lat", False)
-    first, last = edges(weights, natural, forcing, inside).astype(bf16)
-    left = lax.ppermute(last, "lon", eastward)
-    right = lax.ppermute(first, "lon", westward)
-    pushes = push(weights, forcing)
-    spare = jnp.zeros((FIELDS, tiles * 128 - cols - 2 * STRIP, rows), bf16)
-    halo = jnp.concatenate([right, spare, left], axis=1).astype(f32)
-    fields = arrange(natural, pushes, halo, inside, tiles)
-    low = lax.ppermute(fields[:, :, rows - STRIP :].astype(bf16), "lat", northward).astype(f32)
-    high = lax.ppermute(fields[:, :, :STRIP].astype(bf16), "lat", southward).astype(f32)
+    first, last = edges(thickness, natural, forcing, inside)
+    west = lax.ppermute(last, "lon", eastward)
+    east = lax.ppermute(first, "lon", westward)
+    pushes = push(thickness, forcing)
+    bands = range(rows // 128)
+    arranged = [arrange(natural, pushes, east, west, inside, tiles, at) for at in bands]
+    high = lax.ppermute(arranged[0][1], "lat", southward)
+    low = lax.ppermute(arranged[-1][2], "lat", northward)
+    fields = [band[0] for band in arranged]
     wide_rows = lat * rows - TOP + jnp.arange(TOP + rows + 32, dtype=jnp.int32)
     wide_sines, _ = cycle_geometry(wide_rows, cycles)
     spin = (time_step * coriolis_scale) * wide_sines
@@ -488,15 +576,14 @@
     retained = orders3[:, None, :, None] < cycle_length[None, None, None, :]
     weighted = jnp.where(retained, spectra * weight_lat, 0.0).astype(bf16)
     weighted = weighted.reshape(owned * 2 * GROUP, rows)
-    mine = lax.psum_scatter(weighted, "lon", scatter_dimension=0, tiled=True)
-    mine = lax.all_to_all(mine, "lat", 0, 0, tiled=True)
-
-    mine = mine.reshape(lat_parts, groups * 2 * GROUP, rows)
+    mine = lax.all_to_all(weighted, ("lon", "lat"), 0, 0, tiled=True)
+    mine = mine.reshape(lon_parts, lat_parts, groups * 2 * GROUP, rows).astype(f32).sum(axis=0)
+
     flip = jnp.asarray(np.eye(rows)[::-1].astype(bf16))
     hp = lat_parts // 2
-    south = mine[:hp].astype(f32)
-    north_side = jnp.dot(mine[hp:][::-1], flip, preferred_element_type=f32)
-    folded = jnp.stack([south + north_side, south - north_side]).astype(bf16)
+    south = mine[:hp]
+    north_side = jnp.dot(mine[hp:][::-1].astype(bf16), flip, preferred_element_type=f32)
+    folded = jnp.stack([south + north_side, south - north_side])
     folded = folded.reshape(2, hp, groups, 2 * GROUP, rows).transpose(2, 0, 3, 1, 4)
     folded = folded.reshape(groups, 4 * GROUP, hp * rows)
 
@@ -519,8 +606,8 @@
         ),
         axis=1,
     )
-    degree_load = jnp.pad(load_factor, (0, NCHUNK * CHUNK - LMAX)).reshape(NCHUNK, 1, CHUNK, 1)
-    degree_load = jnp.broadcast_to(degree_load, (NCHUNK, 1, CHUNK, GROUP)).reshape(NCHUNK, 1, CROWS)
+    degree_load = jnp.pad(load_factor, (0, HELD * CHUNK - LMAX)).reshape(HELD, 1, CHUNK, 1)
+    degree_load = jnp.broadcast_to(degree_load, (HELD, 1, CHUNK, GROUP)).reshape(HELD, 1, CROWS)
     synth, coeffs = legendre(
         starts,
         folded,
@@ -537,34 +624,58 @@
         (synth[0] - synth[1]).astype(bf16), flip, preferred_element_type=f32
     ).astype(bf16)[::-1]
     share = LMAX // lat_parts
-    coeffs = coeffs.reshape(groups, NCHUNK, 2, CHUNK, GROUP).transpose(0, 2, 4, 1, 3)
-    coeffs = coeffs.reshape(groups * 2 * GROUP, NCHUNK * CHUNK)[:, :LMAX]
+    coeffs = coeffs.reshape(groups, HELD, 2, CHUNK, GROUP).transpose(0, 2, 4, 1, 3)
+    coeffs = coeffs.reshape(groups * 2 * GROUP, HELD * CHUNK)[:, :LMAX]
     coeffs = coeffs.reshape(groups * 2 * GROUP, lat_parts, share).transpose(1, 0, 2).astype(bf16)
-    packet = jnp.concatenate([jnp.concatenate([south, north_side]), coeffs], axis=2)
-    packet = lax.all_to_all(packet.reshape(lat_parts * groups * 2 * GROUP, rows + share), "lat", 0, 0, tiled=True)
-    packet = lax.all_gather(packet, "lon", axis=0, tiled=True)
-    synthesis = packet[:, :rows].reshape(owned, 2, GROUP, rows).astype(f32)
-
+    synth = jnp.concatenate([south, north_side]).reshape(lat_parts * groups * 2 * GROUP, rows)
+    synth = lax.all_to_all(synth, "lat", 0, 0, tiled=True)
+    def sectors(piece):
+        held = [(lon, piece)]
+        for shift in range(1, lon_parts):
+            pairs = [(i, (i + shift) % lon_parts) for i in range(lon_parts)]
+            held.append(((lon - shift) % lon_parts, lax.ppermute(piece, "lon", pairs)))
+        return held
+
+    per_sector = lat_parts * groups
+    sector_waves = jnp.asarray(table.reshape(lon_parts, per_sector * 2 * GROUP, cols))
+    sal_field = jnp.zeros((cols, rows), f32)
     gain = jnp.where(orders3 == 0, 1.0, 2.0)[:, :, None]
-    synthesis = jnp.stack(
-        [
-            gain * (turn_cos * synthesis[:, 0] - turn_sin * synthesis[:, 1]),
-            gain * (turn_sin * synthesis[:, 0] + turn_cos * synthesis[:, 1]),
-        ],
-        axis=1,
-    ).astype(bf16).reshape(owned * 2 * GROUP, rows)
-    sal_field = lax.dot_general(
-        jnp.asarray(table), synthesis, (((0,), (0,)), ((), ())), preferred_element_type=f32
-    )
-
+    cos_gain, sin_gain = gain * turn_cos, gain * turn_sin
+    pieces = sectors(synth)
+    for source, piece in pieces:
+        own = lambda x: lax.dynamic_slice_in_dim(x, source * per_sector, per_sector, 0)
+        cos_own, sin_own = own(cos_gain), own(sin_gain)
+        piece = piece.reshape(per_sector, 2, GROUP, rows).astype(f32)
+        piece = jnp.stack(
+            [
+                cos_own * piece[:, 0] - sin_own * piece[:, 1],
+                sin_own * piece[:, 0] + cos_own * piece[:, 1],
+            ],
+            axis=1,
+        ).astype(bf16).reshape(per_sector * 2 * GROUP, rows)
+        waves = lax.dynamic_index_in_dim(sector_waves, source, 0, keepdims=False)
+        sal_field = sal_field + lax.dot_general(
+            waves, piece, (((0,), (0,)), ((), ())), preferred_element_type=f32
+        )
+
+    coeffs = coeffs.reshape(lat_parts * groups * 2 * GROUP, share)
+    coeffs, _ = lax.optimization_barrier((coeffs, synth))
+    coeffs = lax.all_to_all(coeffs, "lat", 0, 0, tiled=True)
+    coeffs, _ = lax.optimization_barrier((coeffs, [piece for _, piece in pieces]))
     per_owner = LMAX // lon_parts
     own_slots = lax.dynamic_slice(slot_order, (lon * per_owner,), (per_owner,))
-    found = own_slots[:, None] == orders3.reshape(-1)[None, :]
-    by_order = packet[:, rows:].reshape(owned, 2, GROUP, share).transpose(1, 0, 2, 3)
-    by_order = by_order.reshape(2, owned * GROUP, share)
-    load_coeffs = math.sqrt(NLON * cycles) * jnp.einsum(
-        "qm,pmk->pqk", found.astype(bf16), by_order, preferred_element_type=f32
-    )
+    load_coeffs = jnp.zeros((2, per_owner, share), f32)
+    for source, piece in sectors(coeffs):
+        own_orders = lax.dynamic_slice_in_dim(orders3, source * per_sector, per_sector, 0)
+        found = own_slots[:, None] == own_orders.reshape(-1)[None, :]
+        piece = piece.reshape(per_sector, 2, GROUP, share).transpose(1, 0, 2, 3)
+        load_coeffs = load_coeffs + jnp.einsum(
+            "qm,pmk->pqk",
+            found.astype(bf16),
+            piece.reshape(2, per_sector * GROUP, share),
+            preferred_element_type=f32,
+        )
+    load_coeffs = math.sqrt(NLON * cycles) * load_coeffs
     return (height.T, east.T, north.T, load_coeffs, sal_field.T)
 
 

time: 252 us -> 208 us (0.83)
  waiting for transfers between devices: 69.3 us -> 35.4 us
  starting transfers between devices: 11.9 us -> 35.8 us
  other arithmetic: 21.5 us -> 7.36 us
  between operations: 14.4 us -> 1.26 us
  blocking collectives: 10.4 us -> 0 us
  matrix products: 13 us -> 17.2 us
  Pallas kernels: 102 us -> 98.8 us
  local copies, waits for them, and re-layouts: 8.66 us -> 11.5 us
    reduce_scatter x1 -> x0, waiting for transfers between devices: 36.8 us -> none  [local(): mine = lax.psum_scatter(weighted, 'lon', scatter_dimension=0, tiled=True)]
    all_gather x1 -> x0, waiting for transfers between devices: 26.2 us -> none  [local(): packet = lax.all_gather(packet, 'lon', axis=0, tiled=True)]
    all_to_all x1 -> x3, waiting for transfers between devices: 4.42 us -> 23.2 us  [the longest x1 17.1 us: local(): mine = lax.all_to_all(weighted, ('lon', 'lat'), 0, 0, tiled=True)]
    all_to_all x1 -> x3, starting transfers between devices: 3.72 us -> 21.9 us  [the longest x1 15.1 us: local(): mine = lax.all_to_all(weighted, ('lon', 'lat'), 0, 0, tiled=True)]
    all_to_all x1 -> x0, blocking collectives: 10.4 us -> none  [local(): lax.all_to_all(packet.reshape(lat_parts * groups * 2 * GROUP, rows + shar...]
    ppermute x4 -> x10, waiting for transfers between devices: 1.88 us -> 12.2 us  [the longest x6 8.16 us: sectors(): held.append(((lon - shift) % lon_parts, lax.ppermute(piece, 'lon', pairs)))]
    pallas_call x1, Pallas kernels: 32 us -> 24.3 us  [legendre(): pl.pallas_call(legendre_kernel, grid=(groups,), in_specs=[pl.BlockSpec(me...]
    another operation x4 -> x9, other arithmetic: 8.09 us -> 0.62 us
  transfers between devices with their start and end apart: 7 -> 13, of which waited for: 4 -> 5; matrix products, arithmetic and copies ran while one was open for 3% -> 10% of each run, Pallas kernels for 5% -> 9%
where the time goes in v2:
time: 208 us; the launch traced here: 207 us
  Pallas kernels  98.8 us (48%)
  starting transfers between devices  35.8 us (17%)
  waiting for transfers between devices  35.4 us (17%)
  matrix products  17.2 us (8%)
  local copies, waits for them, and re-layouts  11.5 us (6%)
  other arithmetic  7.36 us (4%)
    pallas_call x1, Pallas kernels, ocean(): pl.pallas_call(functools.partial(ocean_kernel, nt, len(fields)), grid=(st...  44.7 us
    pallas_call x1, Pallas kernels, legendre(): pl.pallas_call(legendre_kernel, grid=(groups,), in_specs=[pl.BlockSpec(me...  24.3 us
    pallas_call x2, Pallas kernels, arrange(): pl.pallas_call(functools.partial(arrange_kernel, tiles), grid=(tiles // b...  17.3 us
    all_to_all x1, waiting for transfers between devices, local(): mine = lax.all_to_all(weighted, ('lon', 'lat'), 0, 0, tiled=True)  17.1 us
    all_to_all x1, starting transfers between devices, local(): mine = lax.all_to_all(weighted, ('lon', 'lat'), 0, 0, tiled=True)  15.1 us
    pallas_call x1, Pallas kernels, push(): pl.pallas_call(push_kernel, grid=(-(-cols // width),), in_specs=[pl.Block...  10.7 us
    dot_general x4, matrix products, local(): lax.dot_general(waves, piece, (((0,), (0,)), ((), ())), preferred_element...  10.6 us
    ppermute x6, waiting for transfers between devices, sectors(): held.append(((lon - shift) % lon_parts, lax.ppermute(piece, 'lon', pairs)))  8.16 us
  transfers between devices with their start and end apart: 13, of which 5 were waited for; matrix products, arithmetic and copies ran while one was open for 10% of the time, Pallas kernels for 9%

profile of v2, /device:TPU:0, one launch (start us, length us, event | category | flops | bytes accessed | tf_op | source)
XLA Modules:
  0.0 207.3 jit_solution(18393321328617705198)
XLA Ops:
  0.6 0.6 and_select_fusion.in_ref
  1.2 1.9 edges.1
  3.1 0.9 slice_bitcast_fusion
  4.1 5.1 %collective-permute-start = (bf16[7,24,256]{2,1,0:T(8,128)(2,1)S(1)}, bf16[7,24,256]{2,1,0:T(8,128)(2,1)S(1)}, u32[]{:S(2)}, u32[]{:S(2)}) collective-permute-start(bf16[7,24,256]{2,1,0:T(8,128)(2,1)S(1)} %get-tuple-element.66), channel_id=1, source_target_pairs={{1,0},{2,1},{3,2},{0,3},{5,4},{6,5},{7,6},{4,7},{9,8},{10,9},{11,1... | collective-permute-start | bytes 258056 | tf_op jit(solution)/shard_map/ppermute | solution.py:545
  9.2 10.7 %push.1.p_ref = f32[2,2160,256]{2,1,0:T(8,128)} custom-call(f32[8]{0:T(128)} %thick_ref.3, bf16[2,8,2160,256]{3,2,1,0:T(8,128)(2,1)} %bitcast.122), custom_call_target="tpu_custom_call" | custom-call | flops 17694720 | bytes 22118400 | tf_op jit(solution)/shard_map/push/pallas_call | solution.py:97
  20.3 0.9 dynamic-slice_bitcast_fusion.2
  21.2 0.6 copy-done.4
  21.8 0.6 copy-done.5
  22.5 8.7 %arrange.3 = (f32[7,18,128,128]{3,2,1,0:T(8,128)}, bf16[7,18,24,128]{3,2,1,0:T(8,128)(2,1)}, bf16[7,18,24,128]{3,2,1,0:T(8,128)(2,1)}) custom-call(f32[2160,256]{1,0:T(8,128)} %bitcast.124, f32[2160,256]{1,0:T(8,128)} %bitcast.127, f32[2160,256]{1,0:T(8,128)} %bitcast.130, f32[2160,256]{1,0:T(8,128)} %bitcast.133, s32[2160,256]{1,0:T(8,128)} %bitcast.136, ...), custom_call_target="tpu_custom_call" | custom-call | flops 17694720 | bytes 17694720 | tf_op jit(solution)/shard_map/arrange/pallas_call | solution.py:148
  31.2 1.6 collective-permute-start.2
  32.8 8.6 %arrange.2 = (f32[7,18,128,128]{3,2,1,0:T(8,128)}, bf16[7,18,24,128]{3,2,1,0:T(8,128)(2,1)}, bf16[7,18,24,128]{3,2,1,0:T(8,128)(2,1)}) custom-call(f32[2160,256]{1,0:T(8,128)} %bitcast.125, f32[2160,256]{1,0:T(8,128)} %bitcast.128, f32[2160,256]{1,0:T(8,128)} %bitcast.131, f32[2160,256]{1,0:T(8,128)} %bitcast.134, s32[2160,256]{1,0:T(8,128)} %bitcast.137, ...), custom_call_target="tpu_custom_call" | custom-call | flops 17694720 | bytes 17694720 | tf_op jit(solution)/shard_map/arrange/pallas_call | solution.py:148
  41.4 1.3 collective-permute-start.3
  42.8 0.2 broadcast_compare_fusion
  43.0 0.2 fusion.62
  43.2 4.1 %collective-permute-done.3.refs_4_ = bf16[7,18,24,128]{3,2,1,0:T(8,128)(2,1)S(1)} collective-permute-done((bf16[7,18,24,128]{3,2,1,0:T(8,128)(2,1)}, bf16[7,18,24,128]{3,2,1,0:T(8,128)(2,1)S(1)}, u32[]{:S(2)}, u32[]{:S(2)}) %collective-permute-start.3) | collective-permute-done | bytes 774176 | tf_op jit(solution)/shard_map/ppermute | solution.py:549
  47.3 0.9 broadcast_in_dim.97.refs_2_
  48.2 44.7 %ocean.1 = (f32[2160,256]{1,0:T(8,128)}, f32[2160,256]{1,0:T(8,128)}, f32[2160,256]{1,0:T(8,128)}, bf16[256,2304]{1,0:T(8,128)(2,1)}) custom-call(f32[7,18,128,128]{3,2,1,0:T(8,128)} %get-tuple-element.17.refs_0_, f32[7,18,128,128]{3,2,1,0:T(8,128)} %get-tuple-element.18.refs_1_, f32[320,128]{1,0:T(8,128)} %broadcast_in_dim.97.refs_2_, ...), custom_call_target="tpu_custom_call" | custom-call | tf_op jit(solution)/shard_map/ocean/pallas_call | solution.py:286
  92.9 5.4 %fusion.64 = f32[1536,256]{1,0:T(8,128)S(1)} fusion(bf16[1536,2304]{1,0:T(8,128)(2,1)} %constant.158.clone, bf16[256,2304]{1,0:T(8,128)(2,1)} %get-tuple-element.24), kind=kOutput, calls=%fused_computation.138 | convolution fusion | flops 1811939328 | bytes 9830400 | tf_op jit(solution)/shard_map/dot_general | solution.py:564
  98.3 0.3 multiply_add_fusion
  98.6 0.1 pad_maximum_fusion
  98.8 1.2 select_convert_fusion
  100.0 15.1 %all-to-all-start = ((bf16[32,48,256]{2,1,0:T(8,128)(2,1)}), bf16[32,48,256]{2,1,0:T(8,128)(2,1)S(1)}, u32[]{:S(2)}, u32[]{:S(2)}) async-start(bf16[32,48,256]{2,1,0:T(8,128)(2,1)} %select_convert_fusion), calls=%async_computation | async-start | bytes 1572864 | tf_op jit(solution)/shard_map/all_to_all | solution.py:579
  115.2 0.6 broadcast_multiply_fusion
  115.8 0.7 copy.55.l_ref
  116.6 0.4 fusion.15
  117.0 0.9 select_maximum_fusion.co_ref
  117.9 0.7 multiply_add_fusion.1.z_ref
  118.6 17.1 %all-to-all-done = bf16[32,48,256]{2,1,0:T(8,128)(2,1)S(1)} async-done(((bf16[32,48,256]{2,1,0:T(8,128)(2,1)}), bf16[32,48,256]{2,1,0:T(8,128)(2,1)S(1)}, u32[]{:S(2)}, u32[]{:S(2)}) %all-to-all-start) | async-done | bytes 786464 | tf_op jit(solution)/shard_map/all_to_all | solution.py:579
  135.9 0.2 slice_add_fusion
  136.1 0.1 copy.52
  136.3 0.1 copy.53
  136.5 0.9 reshape.422.w_ref
  137.5 0.6 broadcast_in_dim.101.s_ref
  138.1 24.3 %legendre.1 = (f32[3,32,1024]{2,1,0:T(8,128)}, f32[3,24,2,256]{3,2,1,0:T(2,128)}) custom-call(s32[3]{0:T(128)} %get-tuple-element.50.start_ref, f32[3,32,1024]{2,1,0:T(8,128)} %reshape.422.w_ref, f32[3,8,1024]{2,1,0:T(8,128)} %multiply_add_fusion.1.z_ref, f32[8,1024]{1,0:T(8,128)} %broadcast_in_dim.101.s_ref, f32[3,24,8,128]{3,2,1,0:T(8,128)} %select_maximum_fusion.co_ref, ...), custom_call_target="tpu_custom_call" | custom-call | tf_op jit(solution)/shard_map/legendre/pallas_call | solution.py:426
  162.3 1.2 reshape.429
  163.6 0.2 convolution_convert_fusion
  163.8 0.7 pad_maximum_fusion.1
  164.5 3.4 %all-to-all-start.1 = ((bf16[8,48,256]{2,1,0:T(8,128)(2,1)}), bf16[8,48,256]{2,1,0:T(8,128)(2,1)S(1)}, u32[]{:S(2)}, u32[]{:S(2)}) async-start(bf16[8,48,256]{2,1,0:T(8,128)(2,1)} %pad_maximum_fusion.1), calls=%async_computation.1 | async-start | bytes 393216 | tf_op jit(solution)/shard_map/all_to_all | solution.py:631
  168.4 0.8 dynamic_slice.48
  169.2 0.2 copy.56
  169.5 0.3 copy.57
  169.8 0.2 reshape.427
  170.0 0.1 convert_element_type.169
  170.1 0.7 copy.58
  170.8 3.4 %all-to-all-done.1 = bf16[8,48,256]{2,1,0:T(8,128)(2,1)S(1)} async-done(((bf16[8,48,256]{2,1,0:T(8,128)(2,1)}), bf16[8,48,256]{2,1,0:T(8,128)(2,1)S(1)}, u32[]{:S(2)}, u32[]{:S(2)}) %all-to-all-start.1) | async-done | bytes 196640 | tf_op jit(solution)/shard_map/all_to_all | solution.py:631
  174.1 1.8 collective-permute-start.5
  175.9 0.3 collective-permute-start.4
  176.2 3.4 %all-to-all-start.2 = ((bf16[8,48,90]{2,1,0:T(8,128)(2,1)}), bf16[8,48,90]{2,1,0:T(8,128)(2,1)S(1)}, u32[]{:S(2)}, u32[]{:S(2)}) async-start(bf16[8,48,90]{2,1,0:T(8,128)(2,1)} %bitcast.34), calls=%async_computation.2 | async-start | bytes 196608 | tf_op jit(solution)/shard_map/all_to_all | solution.py:663
  179.6 0.1 subtract_convert_fusion.3
  179.7 2.3 %fusion.3 = f32[256,2160]{0,1:T(8,128)S(1)} fusion(bf16[384,256]{1,0:T(8,128)(2,1)S(1)} %bitcast.147, bf16[4,384,2160]{2,1,0:T(8,128)(2,1)} %constant.161.clone, s32[]{:T(128)S(6)} %select_n.138), kind=kOutput, calls=%fused_computation.6 | convolution fusion | flops 424673280 | bytes 4079620 | tf_op jit(solution)/shard_map/dot_general | solution.py:657
  182.0 2.7 %all-to-all-done.2 = bf16[8,48,90]{2,1,0:T(8,128)(2,1)S(1)} async-done(((bf16[8,48,90]{2,1,0:T(8,128)(2,1)}), bf16[8,48,90]{2,1,0:T(8,128)(2,1)S(1)}, u32[]{:S(2)}, u32[]{:S(2)}) %all-to-all-start.2) | async-done | bytes 69152 | tf_op jit(solution)/shard_map/all_to_all | solution.py:663
  184.7 8.2 %collective-permute-done.5 = bf16[384,256]{1,0:T(8,128)(2,1)S(1)} collective-permute-done((bf16[384,256]{1,0:T(8,128)(2,1)S(1)}, bf16[384,256]{1,0:T(8,128)(2,1)S(1)}, u32[]{:S(2)}, u32[]{:S(2)}) %collective-permute-start.5) | collective-permute-done | bytes 196640 | tf_op jit(solution)/shard_map/ppermute | solution.py:636
  192.8 3.8 %collective-permute-start.9 = (bf16[384,90]{1,0:T(8,128)(2,1)S(1)}, bf16[384,90]{1,0:T(8,128)(2,1)S(1)}, u32[]{:S(2)}, u32[]{:S(2)}) collective-permute-start(bf16[384,90]{1,0:T(8,128)(2,1)S(1)} %bitcast.155), channel_id=1, source_target_pairs={{0,3},{1,0},{2,1},{3,2},{4,7},{5,4},{6,5},{7,6},{8,11},{9,8},{10,9... | collective-permute-start | bytes 207368 | tf_op jit(solution)/shard_map/ppermute | solution.py:636
  196.8 0.1 subtract_convert_fusion
  197.0 0.1 subtract_convert_fusion.1
  197.1 0.1 subtract_convert_fusion.2
  197.3 2.3 %convolution_add_fusion.2 = f32[256,2160]{0,1:T(8,128)S(1)} fusion(f32[256,2160]{0,1:T(8,128)S(1)} %fusion.3, bf16[384,256]{1,0:T(8,128)(2,1)S(1)} %bitcast.146, bf16[4,384,2160]{2,1,0:T(8,128)(2,1)} %constant.161.clone, s32[]{:T(128)S(6)} %select_n.139), kind=kOutput, calls=%fused_computation.2 | convolution fusion | flops 425226240 | bytes 6291460 | tf_op jit(solution)/shard_map/dot_general | solution.py:657
  199.6 2.3 %convolution_add_fusion.1 = f32[256,2160]{0,1:T(8,128)S(1)} fusion(f32[256,2160]{0,1:T(8,128)S(1)} %convolution_add_fusion.2, bf16[384,256]{1,0:T(8,128)(2,1)S(1)} %bitcast.145, bf16[4,384,2160]{2,1,0:T(8,128)(2,1)} %constant.161.clone, s32[]{:T(128)S(6)} %select_n.140), kind=kOutput, calls=%fused_computation.1 | convolution fusion | flops 425226240 | bytes 6291460 | tf_op jit(solution)/shard_map/dot_general | solution.py:657
  201.9 3.7 %convolution_add_fusion = f32[256,2160]{0,1:T(8,128)} fusion(f32[256,2160]{0,1:T(8,128)S(1)} %convolution_add_fusion.1, bf16[384,256]{1,0:T(8,128)(2,1)S(1)} %bitcast.144, bf16[4,384,2160]{2,1,0:T(8,128)(2,1)} %constant.161.clone, s32[]{:T(128)S(6)} %select_n.141), kind=kOutput, calls=%fused_computation | convolution fusion | flops 425226240 | bytes 6291460 | tf_op jit(solution)/shard_map/dot_general | solution.py:657
  205.6 0.2 fusion.20
  205.8 0.2 convolution_add_fusion.4
  206.1 0.2 fusion.16
  206.3 0.2 fusion.11
  206.5 0.8 copy.65
  (71 shorter events, 1.8 us)
Async XLA Ops:
  4.1 17.1 %collective-permute-start = (bf16[7,24,256]{2,1,0:T(8,128)(2,1)S(1)}, bf16[7,24,256]{2,1,0:T(8,128)(2,1)S(1)}, u32[]{:S(2)}, u32[]{:S(2)}) collective-permute-start(bf16[7,24,256]{2,1,0:T(8,128)(2,1)S(1)} %get-tuple-element.66), channel_id=1, source_target_pairs={{1,0},{2,1},{3,2},{0,3},{5,4},{6,5},{7,6},{4,7},{9,8},{10,9},{11,1... | collective-permute-start | bytes 258056 | tf_op jit(solution)/shard_map/ppermute | solution.py:545
  9.2 10.8 %copy-start.8 = (s32[720]{0:T(1024)S(1)}, s32[720]{0:T(1024)}, u32[]{:S(2)}) copy-start(s32[720]{0:T(1024)} %param.25) | copy-start | bytes 8644
  9.2 10.8 %copy-start.10 = (f32[64]{0:T(128)S(1)}, f32[64]{0:T(128)}, u32[]{:S(2)}) copy-start(f32[64]{0:T(128)} %param.26) | copy-start | bytes 772
  9.2 12.0 %collective-permute-start.1 = (bf16[7,24,256]{2,1,0:T(8,128)(2,1)S(1)}, bf16[7,24,256]{2,1,0:T(8,128)(2,1)S(1)}, u32[]{:S(2)}, u32[]{:S(2)}) collective-permute-start(bf16[7,24,256]{2,1,0:T(8,128)(2,1)S(1)} %get-tuple-element.65), channel_id=1, source_target_pairs={{0,1},{1,2},{2,3},{3,0},{4,5},{5,6},{6,7},{7,4},{8,9},{9,10},{10,1... | collective-permute-start | bytes 258056 | tf_op jit(solution)/shard_map/ppermute | solution.py:544
  21.2 0.6 copy-start.4
  21.8 0.6 copy-start.5
  31.1 11.6 %copy-start.3 = (s32[96,8]{1,0:T(8,128)S(1)}, s32[96,8]{1,0:T(8,128)}, u32[]{:S(2)}) copy-start(s32[96,8]{1,0:T(8,128)} %constant.157.clone) | copy-start | bytes 9220
  31.1 11.6 %copy-start.9 = (s32[256]{0:T(256)S(1)}, s32[256]{0:T(256)}, u32[]{:S(2)}) copy-start(s32[256]{0:T(256)} %param.23) | copy-start | bytes 3076
  31.1 11.8 %copy-start.7 = (f32[96,8]{1,0:T(8,128)S(1)}, f32[96,8]{1,0:T(8,128)}, u32[]{:S(2)}) copy-start(f32[96,8]{1,0:T(8,128)} %constant.167) | copy-start | bytes 9220
  31.2 12.0 %collective-permute-start.2 = (bf16[7,18,24,128]{3,2,1,0:T(8,128)(2,1)}, bf16[7,18,24,128]{3,2,1,0:T(8,128)(2,1)S(1)}, u32[]{:S(2)}, u32[]{:S(2)}) collective-permute-start(bf16[7,18,24,128]{3,2,1,0:T(8,128)(2,1)} %get-tuple-element.19), channel_id=1, source_target_pairs={{0,4},{4,8},{8,12},{12,16},{16,20},{20,24},{24,28},{1,5},{5,9},{9,... | collective-permute-start | bytes 2322440 | tf_op jit(solution)/shard_map/ppermute | solution.py:550
  41.4 5.9 %collective-permute-start.3 = (bf16[7,18,24,128]{3,2,1,0:T(8,128)(2,1)}, bf16[7,18,24,128]{3,2,1,0:T(8,128)(2,1)S(1)}, u32[]{:S(2)}, u32[]{:S(2)}) collective-permute-start(bf16[7,18,24,128]{3,2,1,0:T(8,128)(2,1)} %get-tuple-element.20), channel_id=1, source_target_pairs={{4,0},{8,4},{12,8},{16,12},{20,16},{24,20},{28,24},{5,1},{9,5},{13... | collective-permute-start | bytes 2322440 | tf_op jit(solution)/shard_map/ppermute | solution.py:549
  43.2 5.0 %copy-start = (bf16[7,18,24,128]{3,2,1,0:T(8,128)(2,1)}, bf16[7,18,24,128]{3,2,1,0:T(8,128)(2,1)S(1)}, u32[]{:S(2)}) copy-start(bf16[7,18,24,128]{3,2,1,0:T(8,128)(2,1)S(1)} %collective-permute-done.2.refs_3_) | copy-start | bytes 2322436
  47.3 1.0 copy-start.1
  100.0 35.9 %copy-start.2 = (bf16[256,256,1]{1,0,2:T(8,128)(2,1)S(1)}, bf16[256,256,1]{1,0,2:T(8,128)(2,1)}, u32[]{:S(2)}) copy-start(bf16[256,256,1]{1,0,2:T(8,128)(2,1)} %constant.168) | copy-start | bytes 393220
  100.0 35.7 %all-to-all-start = ((bf16[32,48,256]{2,1,0:T(8,128)(2,1)}), bf16[32,48,256]{2,1,0:T(8,128)(2,1)S(1)}, u32[]{:S(2)}, u32[]{:S(2)}) async-start(bf16[32,48,256]{2,1,0:T(8,128)(2,1)} %select_convert_fusion), calls=%async_computation | async-start | bytes 1572864 | tf_op jit(solution)/shard_map/all_to_all | solution.py:579
  162.3 6.8 %copy-start.6 = (f32[3,24,2,256]{3,2,1,0:T(2,128)S(1)}, f32[3,24,2,256]{3,2,1,0:T(2,128)}, u32[]{:S(2)}) copy-start(f32[3,24,2,256]{3,2,1,0:T(2,128)} %get-tuple-element.25) | copy-start | bytes 442372
  164.5 9.6 %all-to-all-start.1 = ((bf16[8,48,256]{2,1,0:T(8,128)(2,1)}), bf16[8,48,256]{2,1,0:T(8,128)(2,1)S(1)}, u32[]{:S(2)}, u32[]{:S(2)}) async-start(bf16[8,48,256]{2,1,0:T(8,128)(2,1)} %pad_maximum_fusion.1), calls=%async_computation.1 | async-start | bytes 393216 | tf_op jit(solution)/shard_map/all_to_all | solution.py:631
  174.1 10.6 %collective-permute-start.6 = (bf16[384,256]{1,0:T(8,128)(2,1)S(1)}, bf16[384,256]{1,0:T(8,128)(2,1)S(1)}, u32[]{:S(2)}, u32[]{:S(2)}) collective-permute-start(bf16[384,256]{1,0:T(8,128)(2,1)S(1)} %bitcast.148), channel_id=1, source_target_pairs={{0,3},{1,0},{2,1},{3,2},{4,7},{5,4},{6,5},{7,6},{8,11},{9,8},{10,9... | collective-permute-start | bytes 589832 | tf_op jit(solution)/shard_map/ppermute | solution.py:636
  174.1 18.7 %collective-permute-start.5 = (bf16[384,256]{1,0:T(8,128)(2,1)S(1)}, bf16[384,256]{1,0:T(8,128)(2,1)S(1)}, u32[]{:S(2)}, u32[]{:S(2)}) collective-permute-start(bf16[384,256]{1,0:T(8,128)(2,1)S(1)} %bitcast.149), channel_id=1, source_target_pairs={{0,2},{1,3},{2,0},{3,1},{4,6},{5,7},{6,4},{7,5},{8,10},{9,11},{10,... | collective-permute-start | bytes 589832 | tf_op jit(solution)/shard_map/ppermute | solution.py:636
  175.9 17.0 %collective-permute-start.4 = (bf16[384,256]{1,0:T(8,128)(2,1)S(1)}, bf16[384,256]{1,0:T(8,128)(2,1)S(1)}, u32[]{:S(2)}, u32[]{:S(2)}) collective-permute-start(bf16[384,256]{1,0:T(8,128)(2,1)S(1)} %bitcast.150), channel_id=1, source_target_pairs={{0,1},{1,2},{2,3},{3,0},{4,5},{5,6},{6,7},{7,4},{8,9},{9,10},{10,1... | collective-permute-start | bytes 589832 | tf_op jit(solution)/shard_map/ppermute | solution.py:636
  176.2 8.5 %all-to-all-start.2 = ((bf16[8,48,90]{2,1,0:T(8,128)(2,1)}), bf16[8,48,90]{2,1,0:T(8,128)(2,1)S(1)}, u32[]{:S(2)}, u32[]{:S(2)}) async-start(bf16[8,48,90]{2,1,0:T(8,128)(2,1)} %bitcast.34), calls=%async_computation.2 | async-start | bytes 196608 | tf_op jit(solution)/shard_map/all_to_all | solution.py:663
  192.8 13.0 %collective-permute-start.7 = (bf16[384,90]{1,0:T(8,128)(2,1)S(1)}, bf16[384,90]{1,0:T(8,128)(2,1)S(1)}, u32[]{:S(2)}, u32[]{:S(2)}) collective-permute-start(bf16[384,90]{1,0:T(8,128)(2,1)S(1)} %bitcast.154), channel_id=1, source_target_pairs={{0,1},{1,2},{2,3},{3,0},{4,5},{5,6},{6,7},{7,4},{8,9},{9,10},{10,1... | collective-permute-start | bytes 207368 | tf_op jit(solution)/shard_map/ppermute | solution.py:636
  192.8 13.2 %collective-permute-start.9 = (bf16[384,90]{1,0:T(8,128)(2,1)S(1)}, bf16[384,90]{1,0:T(8,128)(2,1)S(1)}, u32[]{:S(2)}, u32[]{:S(2)}) collective-permute-start(bf16[384,90]{1,0:T(8,128)(2,1)S(1)} %bitcast.155), channel_id=1, source_target_pairs={{0,3},{1,0},{2,1},{3,2},{4,7},{5,4},{6,5},{7,6},{8,11},{9,8},{10,9... | collective-permute-start | bytes 207368 | tf_op jit(solution)/shard_map/ppermute | solution.py:636
  196.7 9.6 %collective-permute-start.8 = (bf16[384,90]{1,0:T(8,128)(2,1)S(1)}, bf16[384,90]{1,0:T(8,128)(2,1)S(1)}, u32[]{:S(2)}, u32[]{:S(2)}) collective-permute-start(bf16[384,90]{1,0:T(8,128)(2,1)S(1)} %bitcast.156), channel_id=1, source_target_pairs={{0,2},{1,3},{2,0},{3,1},{4,6},{5,7},{6,4},{7,5},{8,10},{9,11},{10,... | collective-permute-start | bytes 207368 | tf_op jit(solution)/shard_map/ppermute | solution.py:636

commit v3 on v2

--- a/solution.py
+++ b/solution.py
@@ -25,6 +25,7 @@
 TOP = 32
 BT = 3
 FIELDS = 7
+WIDE = 4
 GROUP = 8
 CHUNK = 32
 NCHUNK = -(-LMAX // CHUNK)
@@ -113,7 +114,7 @@
 
 def arrange_kernel(
     tiles, h_ref, e_ref, n_ref, d_ref, m_ref, p_ref, east_ref, west_ref, in_ref,
-    out_ref, first_ref, last_ref, halo_ref,
+    wide_ref, short_ref, first_ref, last_ref, halo_ref,
 ):
     lanes = h_ref.shape[0] // tiles
 
@@ -124,8 +125,8 @@
             halo_ref[v, :STRIP, :] = east_ref[v].astype(jnp.float32)
             halo_ref[v, halo_ref.shape[1] - STRIP :, :] = west_ref[v].astype(jnp.float32)
 
-    for b in range(out_ref.shape[1]):
-        t = pl.program_id(0) * out_ref.shape[1] + b
+    for b in range(wide_ref.shape[1]):
+        t = pl.program_id(0) * wide_ref.shape[1] + b
         rows = pl.ds(t, lanes, tiles)
         fields = (
             0.3 * h_ref[rows, :], e_ref[rows, :], n_ref[rows, :], d_ref[rows, :],
@@ -134,7 +135,10 @@
         for v, field in enumerate(fields):
             rest = halo_ref[v, pl.ds(t, 128 - lanes, tiles), :]
             turned = jnp.concatenate([field, rest], axis=0).T
-            out_ref[v, b] = turned
+            if v < WIDE:
+                wide_ref[v, b] = turned
+            else:
+                short_ref[v - WIDE, b] = turned.astype(jnp.bfloat16)
             first_ref[v, b] = turned[:STRIP].astype(jnp.bfloat16)
             last_ref[v, b] = turned[128 - STRIP :].astype(jnp.bfloat16)
 
@@ -142,8 +146,10 @@
 def arrange(fields, pushes, east, west, inside, tiles, at):
     cols, rows = fields[0].shape
     block = BT if tiles % BT == 0 else 1
-    edge = jax.ShapeDtypeStruct((FIELDS, tiles, STRIP, 128), jnp.bfloat16)
-    out_block = lambda n: pl.BlockSpec((FIELDS, block, n, 128), lambda g: (0, g, 0, 0))
+    shape = lambda v, n, dtype: jax.ShapeDtypeStruct((v, tiles, n, 128), dtype)
+    outs = [shape(WIDE, 128, jnp.float32), shape(FIELDS - WIDE, 128, jnp.bfloat16)]
+    outs += [shape(FIELDS, STRIP, jnp.bfloat16)] * 2
+    out_block = lambda x: pl.BlockSpec((x.shape[0], block) + x.shape[2:], lambda g: (0, g, 0, 0))
     halo_block = pl.BlockSpec((FIELDS, STRIP, 128), lambda g: (0, 0, at))
     return pl.pallas_call(
         functools.partial(arrange_kernel, tiles),
@@ -152,8 +158,8 @@
         + [pl.BlockSpec((2, cols, 128), lambda g: (0, 0, at))]
         + [halo_block] * 2
         + [pl.BlockSpec((1, 128), lambda g: (0, at))],
-        out_specs=[out_block(128), out_block(STRIP), out_block(STRIP)],
-        out_shape=[jax.ShapeDtypeStruct((FIELDS, tiles, 128, 128), jnp.float32), edge, edge],
+        out_specs=[out_block(x) for x in outs],
+        out_shape=outs,
         scratch_shapes=[pltpu.VMEM((FIELDS, tiles * 128 - cols, 128), jnp.float32)],
         compiler_params=pltpu.CompilerParams(vmem_limit_bytes=VMEM_LIMIT),
         cost_estimate=pl.CostEstimate(
@@ -164,8 +170,10 @@
 
 
 def ocean_kernel(nt, parts, *refs):
-    field_refs, refs = refs[:parts], refs[parts:]
-    spin_ref, low_ref, high_ref, ho_ref, eo_ref, no_ref, lo_ref, *refs = refs
+    field_refs, refs = refs[: 2 * parts], refs[2 * parts :]
+    spin_ref, *refs = refs
+    low_ref, high_ref, *refs = refs
+    ho_ref, eo_ref, no_ref, lo_ref, *refs = refs
     H, E, N, PE, PN, K, D, A, FE, FN = refs
     step = pl.program_id(0)
     block = field_refs[0].shape[1]
@@ -189,11 +197,14 @@
     def ingest():
         for b in range(block):
             t = step * block + b
-            for part, ref in enumerate(field_refs):
+            both = lambda refs: [
+                ref[v, b].astype(jnp.float32) for ref in refs for v in range(ref.shape[0])
+            ]
+            for part in range(parts):
                 where = slice(TOP + part * 128, TOP + (part + 1) * 128)
-                put(t, where, *[ref[v, b] for v in range(FIELDS)])
-            put(t, slice(TOP - STRIP, TOP), *[low_ref[v, b].astype(jnp.float32) for v in range(FIELDS)])
-            put(t, slice(TOP + rows, TOP + rows + STRIP), *[high_ref[v, b].astype(jnp.float32) for v in range(FIELDS)])
+                put(t, where, *both(field_refs[2 * part : 2 * part + 2]))
+            put(t, slice(TOP - STRIP, TOP), *both([low_ref]))
+            put(t, slice(TOP + rows, TOP + rows + STRIP), *both([high_ref]))
 
     @pl.when(step == nt // block - 1)
     def run():
@@ -235,9 +246,9 @@
 
             def one(substep, carry):
                 close(FE, tiles)
-                lax.fori_loop(0, nt, raise_height, 0)
+                lax.fori_loop(0, nt, raise_height, 0, unroll=BT)
                 close(H, tiles)
-                lax.fori_loop(0, nt, turn, 0)
+                lax.fori_loop(0, nt, turn, 0, unroll=BT)
                 return carry
 
             lax.fori_loop(0, count, one, 0)
@@ -267,14 +278,14 @@
 
 
 def ocean(cols, fields, spin, low, high):
-    nt, rows = fields[0].shape[1], 128 * len(fields)
+    nt, rows = fields[0].shape[1], 64 * len(fields)
     block = BT if nt % BT == 0 else 1
     whole = lambda shape: pl.BlockSpec(
         shape, lambda g: (0,) * len(shape), pipeline_mode=pl.Buffered(1)
     )
     steps = nt // block
-    by_tile = lambda n: pl.BlockSpec(
-        (FIELDS, block, n, 128), lambda g: (0, jnp.minimum(g, steps - 1), 0, 0)
+    by_tile = lambda x: pl.BlockSpec(
+        (x.shape[0], block) + x.shape[2:], lambda g: (0, jnp.minimum(g, steps - 1), 0, 0)
     )
     band = lambda g: jnp.clip(g - (steps - 1), 0, rows // 128 - 1)
     out_block = pl.BlockSpec((cols, 128), lambda g: (0, band(g)))
@@ -284,9 +295,11 @@
     plain = pltpu.VMEM((nt, TOP + rows + 32, 128), jnp.float32)
     ringed = pltpu.VMEM((nt + 2, TOP + rows + 32, 128), jnp.float32)
     return pl.pallas_call(
-        functools.partial(ocean_kernel, nt, len(fields)),
+        functools.partial(ocean_kernel, nt, len(fields) // 2),
         grid=(steps + rows // 128 - 1,),
-        in_specs=[by_tile(128)] * len(fields) + [whole(spin.shape), by_tile(STRIP), by_tile(STRIP)],
+        in_specs=[by_tile(x) for x in fields]
+        + [whole(spin.shape)]
+        + [by_tile(low), by_tile(high)],
         out_specs=[out_block] * 3 + [load_block],
         out_shape=outs,
         scratch_shapes=[ringed] + [plain] * 7 + [ringed, plain],
@@ -546,9 +559,9 @@
     pushes = push(thickness, forcing)
     bands = range(rows // 128)
     arranged = [arrange(natural, pushes, east, west, inside, tiles, at) for at in bands]
-    high = lax.ppermute(arranged[0][1], "lat", southward)
-    low = lax.ppermute(arranged[-1][2], "lat", northward)
-    fields = [band[0] for band in arranged]
+    high = lax.ppermute(arranged[0][2], "lat", southward)
+    low = lax.ppermute(arranged[-1][3], "lat", northward)
+    fields = [x for band in arranged for x in band[:2]]
     wide_rows = lat * rows - TOP + jnp.arange(TOP + rows + 32, dtype=jnp.int32)
     wide_sines, _ = cycle_geometry(wide_rows, cycles)
     spin = (time_step * coriolis_scale) * wide_sines

time: 208 us -> 204 us (0.981)
  Pallas kernels: 98.8 us -> 94.6 us
    pallas_call x1, Pallas kernels: 44.7 us -> 41.7 us  [ocean(): pl.pallas_call(functools.partial(ocean_kernel, nt, len(fields) // 2), gri...]
where the time goes in v3:
time: 204 us; the launch traced here: 203 us
  Pallas kernels  94.6 us (46%)
  starting transfers between devices  35.9 us (18%)
  waiting for transfers between devices  35.2 us (17%)
  matrix products  17.2 us (8%)
  local copies, waits for them, and re-layouts  11.5 us (6%)
  other arithmetic  7.29 us (4%)
    pallas_call x1, Pallas kernels, ocean(): pl.pallas_call(functools.partial(ocean_kernel, nt, len(fields) // 2), gri...  41.7 us
    pallas_call x1, Pallas kernels, legendre(): pl.pallas_call(legendre_kernel, grid=(groups,), in_specs=[pl.BlockSpec(me...  24.3 us
    all_to_all x1, waiting for transfers between devices, local(): mine = lax.all_to_all(weighted, ('lon', 'lat'), 0, 0, tiled=True)  17.1 us
    pallas_call x2, Pallas kernels, arrange(): pl.pallas_call(functools.partial(arrange_kernel, tiles), grid=(tiles // b...  16.1 us
    all_to_all x1, starting transfers between devices, local(): mine = lax.all_to_all(weighted, ('lon', 'lat'), 0, 0, tiled=True)  15.1 us
    pallas_call x1, Pallas kernels, push(): pl.pallas_call(push_kernel, grid=(-(-cols // width),), in_specs=[pl.Block...  10.7 us
    dot_general x4, matrix products, local(): lax.dot_general(waves, piece, (((0,), (0,)), ((), ())), preferred_element...  10.6 us
    ppermute x6, waiting for transfers between devices, sectors(): held.append(((lon - shift) % lon_parts, lax.ppermute(piece, 'lon', pairs)))  8.16 us
  transfers between devices with their start and end apart: 13, of which 5 were waited for; matrix products, arithmetic and copies ran while one was open for 10% of the time, Pallas kernels for 9%

profile of v3, /device:TPU:0, one launch (start us, length us, event | category | flops | bytes accessed | tf_op | source)
XLA Modules:
  0.0 203.0 jit_solution(16673792633376567721)
XLA Ops:
  0.6 0.5 and_select_fusion.in_ref
  1.2 1.9 edges.1
  3.1 0.9 slice_bitcast_fusion
  4.0 5.1 %collective-permute-start = (bf16[7,24,256]{2,1,0:T(8,128)(2,1)S(1)}, bf16[7,24,256]{2,1,0:T(8,128)(2,1)S(1)}, u32[]{:S(2)}, u32[]{:S(2)}) collective-permute-start(bf16[7,24,256]{2,1,0:T(8,128)(2,1)S(1)} %get-tuple-element.70), channel_id=1, source_target_pairs={{1,0},{2,1},{3,2},{0,3},{5,4},{6,5},{7,6},{4,7},{9,8},{10,9},{11,1... | collective-permute-start | bytes 258056 | tf_op jit(solution)/shard_map/ppermute | solution.py:558
  9.1 10.7 %push.1.p_ref = f32[2,2160,256]{2,1,0:T(8,128)} custom-call(f32[8]{0:T(128)} %thick_ref.3, bf16[2,8,2160,256]{3,2,1,0:T(8,128)(2,1)} %bitcast.122), custom_call_target="tpu_custom_call" | custom-call | flops 17694720 | bytes 22118400 | tf_op jit(solution)/shard_map/push/pallas_call | solution.py:98
  20.2 0.9 dynamic-slice_bitcast_fusion.2
  21.1 0.6 copy-done.4
  21.7 0.6 copy-done.5
  22.4 8.0 %arrange.3 = (f32[4,18,128,128]{3,2,1,0:T(8,128)}, bf16[3,18,128,128]{3,2,1,0:T(8,128)(2,1)}, bf16[7,18,24,128]{3,2,1,0:T(8,128)(2,1)}, bf16[7,18,24,128]{3,2,1,0:T(8,128)(2,1)}) custom-call(f32[2160,256]{1,0:T(8,128)} %bitcast.124, f32[2160,256]{1,0:T(8,128)} %bitcast.127, f32[2160,256]{1,0:T(8,128)} %bitcast.130, f32[2160,256]{1,0:T(8,128)} %bitcast.133, ...), custom_call_target="tpu_custom_call" | custom-call | flops 17694720 | bytes 17694720 | tf_op jit(solution)/shard_map/arrange/pallas_call | solution.py:154
  30.4 1.6 collective-permute-start.2
  32.0 8.1 %arrange.2 = (f32[4,18,128,128]{3,2,1,0:T(8,128)}, bf16[3,18,128,128]{3,2,1,0:T(8,128)(2,1)}, bf16[7,18,24,128]{3,2,1,0:T(8,128)(2,1)}, bf16[7,18,24,128]{3,2,1,0:T(8,128)(2,1)}) custom-call(f32[2160,256]{1,0:T(8,128)} %bitcast.125, f32[2160,256]{1,0:T(8,128)} %bitcast.128, f32[2160,256]{1,0:T(8,128)} %bitcast.131, f32[2160,256]{1,0:T(8,128)} %bitcast.134, ...), custom_call_target="tpu_custom_call" | custom-call | flops 17694720 | bytes 17694720 | tf_op jit(solution)/shard_map/arrange/pallas_call | solution.py:154
  40.1 1.3 collective-permute-start.3
  41.5 0.2 broadcast_compare_fusion
  41.7 0.2 fusion.62
  41.9 4.1 %collective-permute-done.3.refs_6_ = bf16[7,18,24,128]{3,2,1,0:T(8,128)(2,1)S(1)} collective-permute-done((bf16[7,18,24,128]{3,2,1,0:T(8,128)(2,1)}, bf16[7,18,24,128]{3,2,1,0:T(8,128)(2,1)S(1)}, u32[]{:S(2)}, u32[]{:S(2)}) %collective-permute-start.3) | collective-permute-done | bytes 774176 | tf_op jit(solution)/shard_map/ppermute | solution.py:562
  46.0 0.9 broadcast_in_dim.97.refs_4_
  46.9 41.7 %ocean.1 = (f32[2160,256]{1,0:T(8,128)}, f32[2160,256]{1,0:T(8,128)}, f32[2160,256]{1,0:T(8,128)}, bf16[256,2304]{1,0:T(8,128)(2,1)}) custom-call(f32[4,18,128,128]{3,2,1,0:T(8,128)} %get-tuple-element.19.refs_0_, bf16[3,18,128,128]{3,2,1,0:T(8,128)(2,1)} %get-tuple-element.20.refs_1_, f32[4,18,128,128]{3,2,1,0:T(8,128)} %get-tuple-element.21.refs_2_, ...), custom_call_target="tpu_custom_call" | custom-call | tf_op jit(solution)/shard_map/ocean/pallas_call | solution.py:297
  88.6 5.4 %fusion.64 = f32[1536,256]{1,0:T(8,128)S(1)} fusion(bf16[1536,2304]{1,0:T(8,128)(2,1)} %constant.158.clone, bf16[256,2304]{1,0:T(8,128)(2,1)} %get-tuple-element.28), kind=kOutput, calls=%fused_computation.138 | convolution fusion | flops 1811939328 | bytes 9830400 | tf_op jit(solution)/shard_map/dot_general | solution.py:577
  94.0 0.3 multiply_add_fusion
  94.3 0.1 pad_maximum_fusion
  94.5 1.2 select_convert_fusion
  95.7 15.1 %all-to-all-start = ((bf16[32,48,256]{2,1,0:T(8,128)(2,1)}), bf16[32,48,256]{2,1,0:T(8,128)(2,1)S(1)}, u32[]{:S(2)}, u32[]{:S(2)}) async-start(bf16[32,48,256]{2,1,0:T(8,128)(2,1)} %select_convert_fusion), calls=%async_computation | async-start | bytes 1572864 | tf_op jit(solution)/shard_map/all_to_all | solution.py:592
  110.9 0.6 broadcast_multiply_fusion
  111.5 0.7 copy.55.l_ref
  112.3 0.4 fusion.15
  112.7 0.9 select_maximum_fusion.co_ref
  113.6 0.7 multiply_add_fusion.1.z_ref
  114.3 17.1 %all-to-all-done = bf16[32,48,256]{2,1,0:T(8,128)(2,1)S(1)} async-done(((bf16[32,48,256]{2,1,0:T(8,128)(2,1)}), bf16[32,48,256]{2,1,0:T(8,128)(2,1)S(1)}, u32[]{:S(2)}, u32[]{:S(2)}) %all-to-all-start) | async-done | bytes 786464 | tf_op jit(solution)/shard_map/all_to_all | solution.py:592
  131.6 0.2 slice_add_fusion
  131.8 0.1 copy.52
  132.0 0.1 copy.53
  132.2 0.9 reshape.422.w_ref
  133.2 0.6 broadcast_in_dim.101.s_ref
  133.8 24.3 %legendre.1 = (f32[3,32,1024]{2,1,0:T(8,128)}, f32[3,24,2,256]{3,2,1,0:T(2,128)}) custom-call(s32[3]{0:T(128)} %get-tuple-element.54.start_ref, f32[3,32,1024]{2,1,0:T(8,128)} %reshape.422.w_ref, f32[3,8,1024]{2,1,0:T(8,128)} %multiply_add_fusion.1.z_ref, f32[8,1024]{1,0:T(8,128)} %broadcast_in_dim.101.s_ref, f32[3,24,8,128]{3,2,1,0:T(8,128)} %select_maximum_fusion.co_ref, ...), custom_call_target="tpu_custom_call" | custom-call | tf_op jit(solution)/shard_map/legendre/pallas_call | solution.py:439
  158.0 1.2 reshape.429
  159.3 0.2 convolution_convert_fusion
  159.5 0.7 pad_maximum_fusion.1
  160.2 3.6 %all-to-all-start.1 = ((bf16[8,48,256]{2,1,0:T(8,128)(2,1)}), bf16[8,48,256]{2,1,0:T(8,128)(2,1)S(1)}, u32[]{:S(2)}, u32[]{:S(2)}) async-start(bf16[8,48,256]{2,1,0:T(8,128)(2,1)} %pad_maximum_fusion.1), calls=%async_computation.1 | async-start | bytes 393216 | tf_op jit(solution)/shard_map/all_to_all | solution.py:644
  164.2 0.8 dynamic_slice.48
  165.1 0.2 copy.56
  165.3 0.3 copy.57
  165.6 0.2 reshape.427
  165.8 0.1 convert_element_type.169
  166.0 0.7 copy.58
  166.6 3.2 %all-to-all-done.1 = bf16[8,48,256]{2,1,0:T(8,128)(2,1)S(1)} async-done(((bf16[8,48,256]{2,1,0:T(8,128)(2,1)}), bf16[8,48,256]{2,1,0:T(8,128)(2,1)S(1)}, u32[]{:S(2)}, u32[]{:S(2)}) %all-to-all-start.1) | async-done | bytes 196640 | tf_op jit(solution)/shard_map/all_to_all | solution.py:644
  169.8 1.8 collective-permute-start.5
  171.6 0.3 collective-permute-start.4
  171.9 3.4 %all-to-all-start.2 = ((bf16[8,48,90]{2,1,0:T(8,128)(2,1)}), bf16[8,48,90]{2,1,0:T(8,128)(2,1)S(1)}, u32[]{:S(2)}, u32[]{:S(2)}) async-start(bf16[8,48,90]{2,1,0:T(8,128)(2,1)} %bitcast.34), calls=%async_computation.2 | async-start | bytes 196608 | tf_op jit(solution)/shard_map/all_to_all | solution.py:676
  175.3 0.1 subtract_convert_fusion.3
  175.4 2.3 %fusion.3 = f32[256,2160]{0,1:T(8,128)S(1)} fusion(bf16[384,256]{1,0:T(8,128)(2,1)S(1)} %bitcast.147, bf16[4,384,2160]{2,1,0:T(8,128)(2,1)} %constant.161.clone, s32[]{:T(128)S(6)} %select_n.138), kind=kOutput, calls=%fused_computation.6 | convolution fusion | flops 424673280 | bytes 4079620 | tf_op jit(solution)/shard_map/dot_general | solution.py:670
  177.7 2.7 %all-to-all-done.2 = bf16[8,48,90]{2,1,0:T(8,128)(2,1)S(1)} async-done(((bf16[8,48,90]{2,1,0:T(8,128)(2,1)}), bf16[8,48,90]{2,1,0:T(8,128)(2,1)S(1)}, u32[]{:S(2)}, u32[]{:S(2)}) %all-to-all-start.2) | async-done | bytes 69152 | tf_op jit(solution)/shard_map/all_to_all | solution.py:676
  180.4 8.2 %collective-permute-done.5 = bf16[384,256]{1,0:T(8,128)(2,1)S(1)} collective-permute-done((bf16[384,256]{1,0:T(8,128)(2,1)S(1)}, bf16[384,256]{1,0:T(8,128)(2,1)S(1)}, u32[]{:S(2)}, u32[]{:S(2)}) %collective-permute-start.5) | collective-permute-done | bytes 196640 | tf_op jit(solution)/shard_map/ppermute | solution.py:649
  188.5 3.8 %collective-permute-start.9 = (bf16[384,90]{1,0:T(8,128)(2,1)S(1)}, bf16[384,90]{1,0:T(8,128)(2,1)S(1)}, u32[]{:S(2)}, u32[]{:S(2)}) collective-permute-start(bf16[384,90]{1,0:T(8,128)(2,1)S(1)} %bitcast.155), channel_id=1, source_target_pairs={{0,3},{1,0},{2,1},{3,2},{4,7},{5,4},{6,5},{7,6},{8,11},{9,8},{10,9... | collective-permute-start | bytes 207368 | tf_op jit(solution)/shard_map/ppermute | solution.py:649
  192.5 0.1 subtract_convert_fusion
  192.7 0.1 subtract_convert_fusion.1
  192.8 0.1 subtract_convert_fusion.2
  193.0 2.3 %convolution_add_fusion.2 = f32[256,2160]{0,1:T(8,128)S(1)} fusion(f32[256,2160]{0,1:T(8,128)S(1)} %fusion.3, bf16[384,256]{1,0:T(8,128)(2,1)S(1)} %bitcast.146, bf16[4,384,2160]{2,1,0:T(8,128)(2,1)} %constant.161.clone, s32[]{:T(128)S(6)} %select_n.139), kind=kOutput, calls=%fused_computation.2 | convolution fusion | flops 425226240 | bytes 6291460 | tf_op jit(solution)/shard_map/dot_general | solution.py:670
  195.3 2.3 %convolution_add_fusion.1 = f32[256,2160]{0,1:T(8,128)S(1)} fusion(f32[256,2160]{0,1:T(8,128)S(1)} %convolution_add_fusion.2, bf16[384,256]{1,0:T(8,128)(2,1)S(1)} %bitcast.145, bf16[4,384,2160]{2,1,0:T(8,128)(2,1)} %constant.161.clone, s32[]{:T(128)S(6)} %select_n.140), kind=kOutput, calls=%fused_computation.1 | convolution fusion | flops 425226240 | bytes 6291460 | tf_op jit(solution)/shard_map/dot_general | solution.py:670
  197.6 3.7 %convolution_add_fusion = f32[256,2160]{0,1:T(8,128)} fusion(f32[256,2160]{0,1:T(8,128)S(1)} %convolution_add_fusion.1, bf16[384,256]{1,0:T(8,128)(2,1)S(1)} %bitcast.144, bf16[4,384,2160]{2,1,0:T(8,128)(2,1)} %constant.161.clone, s32[]{:T(128)S(6)} %select_n.141), kind=kOutput, calls=%fused_computation | convolution fusion | flops 425226240 | bytes 6291460 | tf_op jit(solution)/shard_map/dot_general | solution.py:670
  201.3 0.2 fusion.20
  201.5 0.2 convolution_add_fusion.4
  201.8 0.2 fusion.16
  202.0 0.2 fusion.11
  202.2 0.8 copy.65
  (71 shorter events, 1.8 us)
Async XLA Ops:
  4.0 17.1 %collective-permute-start = (bf16[7,24,256]{2,1,0:T(8,128)(2,1)S(1)}, bf16[7,24,256]{2,1,0:T(8,128)(2,1)S(1)}, u32[]{:S(2)}, u32[]{:S(2)}) collective-permute-start(bf16[7,24,256]{2,1,0:T(8,128)(2,1)S(1)} %get-tuple-element.70), channel_id=1, source_target_pairs={{1,0},{2,1},{3,2},{0,3},{5,4},{6,5},{7,6},{4,7},{9,8},{10,9},{11,1... | collective-permute-start | bytes 258056 | tf_op jit(solution)/shard_map/ppermute | solution.py:558
  9.1 10.8 %copy-start.8 = (s32[720]{0:T(1024)S(1)}, s32[720]{0:T(1024)}, u32[]{:S(2)}) copy-start(s32[720]{0:T(1024)} %param.25) | copy-start | bytes 8644
  9.1 10.8 %copy-start.10 = (f32[64]{0:T(128)S(1)}, f32[64]{0:T(128)}, u32[]{:S(2)}) copy-start(f32[64]{0:T(128)} %param.26) | copy-start | bytes 772
  9.1 12.0 %collective-permute-start.1 = (bf16[7,24,256]{2,1,0:T(8,128)(2,1)S(1)}, bf16[7,24,256]{2,1,0:T(8,128)(2,1)S(1)}, u32[]{:S(2)}, u32[]{:S(2)}) collective-permute-start(bf16[7,24,256]{2,1,0:T(8,128)(2,1)S(1)} %get-tuple-element.69), channel_id=1, source_target_pairs={{0,1},{1,2},{2,3},{3,0},{4,5},{5,6},{6,7},{7,4},{8,9},{9,10},{10,1... | collective-permute-start | bytes 258056 | tf_op jit(solution)/shard_map/ppermute | solution.py:557
  21.1 0.6 copy-start.4
  21.7 0.6 copy-start.5
  30.4 11.1 %copy-start.3 = (s32[96,8]{1,0:T(8,128)S(1)}, s32[96,8]{1,0:T(8,128)}, u32[]{:S(2)}) copy-start(s32[96,8]{1,0:T(8,128)} %constant.157.clone) | copy-start | bytes 9220
  30.4 11.1 %copy-start.9 = (s32[256]{0:T(256)S(1)}, s32[256]{0:T(256)}, u32[]{:S(2)}) copy-start(s32[256]{0:T(256)} %param.23) | copy-start | bytes 3076
  30.4 11.3 %copy-start.7 = (f32[96,8]{1,0:T(8,128)S(1)}, f32[96,8]{1,0:T(8,128)}, u32[]{:S(2)}) copy-start(f32[96,8]{1,0:T(8,128)} %constant.167) | copy-start | bytes 9220
  30.4 11.5 %collective-permute-start.2 = (bf16[7,18,24,128]{3,2,1,0:T(8,128)(2,1)}, bf16[7,18,24,128]{3,2,1,0:T(8,128)(2,1)S(1)}, u32[]{:S(2)}, u32[]{:S(2)}) collective-permute-start(bf16[7,18,24,128]{3,2,1,0:T(8,128)(2,1)} %get-tuple-element.23), channel_id=1, source_target_pairs={{0,4},{4,8},{8,12},{12,16},{16,20},{20,24},{24,28},{1,5},{5,9},{9,... | collective-permute-start | bytes 2322440 | tf_op jit(solution)/shard_map/ppermute | solution.py:563
  40.1 5.9 %collective-permute-start.3 = (bf16[7,18,24,128]{3,2,1,0:T(8,128)(2,1)}, bf16[7,18,24,128]{3,2,1,0:T(8,128)(2,1)S(1)}, u32[]{:S(2)}, u32[]{:S(2)}) collective-permute-start(bf16[7,18,24,128]{3,2,1,0:T(8,128)(2,1)} %get-tuple-element.24), channel_id=1, source_target_pairs={{4,0},{8,4},{12,8},{16,12},{20,16},{24,20},{28,24},{5,1},{9,5},{13... | collective-permute-start | bytes 2322440 | tf_op jit(solution)/shard_map/ppermute | solution.py:562
  41.9 5.0 %copy-start = (bf16[7,18,24,128]{3,2,1,0:T(8,128)(2,1)}, bf16[7,18,24,128]{3,2,1,0:T(8,128)(2,1)S(1)}, u32[]{:S(2)}) copy-start(bf16[7,18,24,128]{3,2,1,0:T(8,128)(2,1)S(1)} %collective-permute-done.2.refs_5_) | copy-start | bytes 2322436
  46.0 0.9 copy-start.1
  95.7 35.9 %copy-start.2 = (bf16[256,256,1]{1,0,2:T(8,128)(2,1)S(1)}, bf16[256,256,1]{1,0,2:T(8,128)(2,1)}, u32[]{:S(2)}) copy-start(bf16[256,256,1]{1,0,2:T(8,128)(2,1)} %constant.168) | copy-start | bytes 393220
  95.7 35.7 %all-to-all-start = ((bf16[32,48,256]{2,1,0:T(8,128)(2,1)}), bf16[32,48,256]{2,1,0:T(8,128)(2,1)S(1)}, u32[]{:S(2)}, u32[]{:S(2)}) async-start(bf16[32,48,256]{2,1,0:T(8,128)(2,1)} %select_convert_fusion), calls=%async_computation | async-start | bytes 1572864 | tf_op jit(solution)/shard_map/all_to_all | solution.py:592
  158.0 7.0 %copy-start.6 = (f32[3,24,2,256]{3,2,1,0:T(2,128)S(1)}, f32[3,24,2,256]{3,2,1,0:T(2,128)}, u32[]{:S(2)}) copy-start(f32[3,24,2,256]{3,2,1,0:T(2,128)} %get-tuple-element.29) | copy-start | bytes 442372
  160.2 9.6 %all-to-all-start.1 = ((bf16[8,48,256]{2,1,0:T(8,128)(2,1)}), bf16[8,48,256]{2,1,0:T(8,128)(2,1)S(1)}, u32[]{:S(2)}, u32[]{:S(2)}) async-start(bf16[8,48,256]{2,1,0:T(8,128)(2,1)} %pad_maximum_fusion.1), calls=%async_computation.1 | async-start | bytes 393216 | tf_op jit(solution)/shard_map/all_to_all | solution.py:644
  169.8 10.6 %collective-permute-start.6 = (bf16[384,256]{1,0:T(8,128)(2,1)S(1)}, bf16[384,256]{1,0:T(8,128)(2,1)S(1)}, u32[]{:S(2)}, u32[]{:S(2)}) collective-permute-start(bf16[384,256]{1,0:T(8,128)(2,1)S(1)} %bitcast.148), channel_id=1, source_target_pairs={{0,3},{1,0},{2,1},{3,2},{4,7},{5,4},{6,5},{7,6},{8,11},{9,8},{10,9... | collective-permute-start | bytes 589832 | tf_op jit(solution)/shard_map/ppermute | solution.py:649
  169.8 18.7 %collective-permute-start.5 = (bf16[384,256]{1,0:T(8,128)(2,1)S(1)}, bf16[384,256]{1,0:T(8,128)(2,1)S(1)}, u32[]{:S(2)}, u32[]{:S(2)}) collective-permute-start(bf16[384,256]{1,0:T(8,128)(2,1)S(1)} %bitcast.149), channel_id=1, source_target_pairs={{0,2},{1,3},{2,0},{3,1},{4,6},{5,7},{6,4},{7,5},{8,10},{9,11},{10,... | collective-permute-start | bytes 589832 | tf_op jit(solution)/shard_map/ppermute | solution.py:649
  171.6 17.0 %collective-permute-start.4 = (bf16[384,256]{1,0:T(8,128)(2,1)S(1)}, bf16[384,256]{1,0:T(8,128)(2,1)S(1)}, u32[]{:S(2)}, u32[]{:S(2)}) collective-permute-start(bf16[384,256]{1,0:T(8,128)(2,1)S(1)} %bitcast.150), channel_id=1, source_target_pairs={{0,1},{1,2},{2,3},{3,0},{4,5},{5,6},{6,7},{7,4},{8,9},{9,10},{10,1... | collective-permute-start | bytes 589832 | tf_op jit(solution)/shard_map/ppermute | solution.py:649
  171.9 8.5 %all-to-all-start.2 = ((bf16[8,48,90]{2,1,0:T(8,128)(2,1)}), bf16[8,48,90]{2,1,0:T(8,128)(2,1)S(1)}, u32[]{:S(2)}, u32[]{:S(2)}) async-start(bf16[8,48,90]{2,1,0:T(8,128)(2,1)} %bitcast.34), calls=%async_computation.2 | async-start | bytes 196608 | tf_op jit(solution)/shard_map/all_to_all | solution.py:676
  188.5 13.0 %collective-permute-start.7 = (bf16[384,90]{1,0:T(8,128)(2,1)S(1)}, bf16[384,90]{1,0:T(8,128)(2,1)S(1)}, u32[]{:S(2)}, u32[]{:S(2)}) collective-permute-start(bf16[384,90]{1,0:T(8,128)(2,1)S(1)} %bitcast.154), channel_id=1, source_target_pairs={{0,1},{1,2},{2,3},{3,0},{4,5},{5,6},{6,7},{7,4},{8,9},{9,10},{10,1... | collective-permute-start | bytes 207368 | tf_op jit(solution)/shard_map/ppermute | solution.py:649
  188.5 13.2 %collective-permute-start.9 = (bf16[384,90]{1,0:T(8,128)(2,1)S(1)}, bf16[384,90]{1,0:T(8,128)(2,1)S(1)}, u32[]{:S(2)}, u32[]{:S(2)}) collective-permute-start(bf16[384,90]{1,0:T(8,128)(2,1)S(1)} %bitcast.155), channel_id=1, source_target_pairs={{0,3},{1,0},{2,1},{3,2},{4,7},{5,4},{6,5},{7,6},{8,11},{9,8},{10,9... | collective-permute-start | bytes 207368 | tf_op jit(solution)/shard_map/ppermute | solution.py:649
  192.4 9.6 %collective-permute-start.8 = (bf16[384,90]{1,0:T(8,128)(2,1)S(1)}, bf16[384,90]{1,0:T(8,128)(2,1)S(1)}, u32[]{:S(2)}, u32[]{:S(2)}) collective-permute-start(bf16[384,90]{1,0:T(8,128)(2,1)S(1)} %bitcast.156), channel_id=1, source_target_pairs={{0,2},{1,3},{2,0},{3,1},{4,6},{5,7},{6,4},{7,5},{8,10},{9,11},{10,... | collective-permute-start | bytes 207368 | tf_op jit(solution)/shard_map/ppermute | solution.py:649
